TPU v7x, 32 devices: a whole 2x2x4 slice. The times are simulated.
32 devices in a mesh: section: 4 (over y, core), dp: 8 (over z, x).
Axes of the slice: x: 2, y: 2, z: 4, core: 2. Of those that a mesh axis runs over, the one named last changes fastest.
Arguments:
- tokens: bfloat16 [32, 4, 512, 512], P('dp', 'section'), may hold values from -6 to 6
- doc_ids: int32 [32, 4, 512], P('dp', 'section'), may hold values from 0 to 3, never falling along the last dimension, each value on 1 to 256 neighbouring positions
- reset_flags: int32 [32, 4], P('dp', 'section'), may hold values from 0 to 1, as said below
- attn_gain: bfloat16 [512], replicated, may hold values from 0.5 to 1.5
- w_qkv: bfloat16 [512, 1536], replicated, may hold values from -0.25 to 0.25
- w_attn_out: bfloat16 [512, 512], replicated, may hold values from -0.75 to 0.75
- ffn_gain: bfloat16 [512], replicated, may hold values from 0.5 to 1.5
- w_in: bfloat16 [512, 2048], replicated, may hold values from -0.25 to 0.25
- w_out: bfloat16 [2048, 512], replicated, may hold values from -0.1875 to 0.1875
- write_gain: bfloat16 [512], replicated, may hold values from 0.5 to 1.5
- w_write: bfloat16 [512, 1536], replicated, may hold values from -0.25 to 0.25
- w_write_out: bfloat16 [512, 512], replicated, may hold values from -1 to 1
- init_memory: bfloat16 [64, 512], replicated, may hold values from -6 to 6
- out_grad: bfloat16 [32, 4, 512, 512], P('dp', 'section'), may hold values from -6 to 6
- memory_grad: bfloat16 [32, 4, 64, 512], P('dp', 'section'), may hold values from -6 to 6
Outputs:
- encoded: bfloat16 [32, 4, 512, 512], P('dp', 'section')
- memories: bfloat16 [32, 4, 64, 512], P('dp', 'section')
- tokens_grad: float32 [32, 4, 512, 512], P('dp', 'section')
- attn_gain_grad: float32 [512], replicated
- w_qkv_grad: float32 [512, 1536], replicated
- w_attn_out_grad: float32 [512, 512], replicated
- ffn_gain_grad: float32 [512], replicated
- w_in_grad: float32 [512, 2048], replicated
- w_out_grad: float32 [2048, 512], replicated
- write_gain_grad: float32 [512], replicated
- w_write_grad: float32 [512, 1536], replicated
- w_write_out_grad: float32 [512, 512], replicated
- init_memory_grad: float32 [64, 512], replicated
Inputs may be any that keep to these rules, and one draw needn't show every extreme that they name: `reset_flags`: the first segment of every stream has flag 1; among the 4 streams of each index of dp one has no other flag.
All inputs are finite; a program needn't handle non-finite values.
Results may differ from a plain program's by a relative error of at most 0.014.
Values may be sent and summed in bfloat16 or wider, within the bound.
No kernel may reach another device: no remote copies, remote signals or barrier semaphores. Data moves between devices by JAX's collectives and lax.ppermute only.
A program may use at most 256 MiB of HBM per device.

v0:
```python
import jax
import jax.numpy as jnp
from jax import lax
from jax.sharding import PartitionSpec as P

HEADS = 8
HEAD_DIM = 64


EPS = 1e-06
MASKED = -1000000000.0


def shifted(block, axis, distance):
    devices = range(lax.axis_size(axis))
    route = [(i - distance, i) for i in devices if i - distance in devices]
    return lax.ppermute(block, axis, route)


def norm_rows(values, gain):
    return values * lax.rsqrt(jnp.mean(values * values, axis=-1, keepdims=True) + EPS) * gain


def heads_of(values):
    return values.reshape(values.shape[0], HEADS, HEAD_DIM)


def rows_of(values):
    return values.reshape(values.shape[0], HEADS * HEAD_DIM)


def product(left, right):
    return jnp.dot(left, right, preferred_element_type=jnp.float32)


def attend(queries, keys, values, allowed):
    scale = HEAD_DIM ** (-0.5)
    scores = (
        jnp.einsum(
            "qhd,khd->hqk", heads_of(queries), heads_of(keys), preferred_element_type=jnp.float32
        )
        * scale
    )
    attn_probs = jax.nn.softmax(jnp.where(allowed[None], scores, MASKED), axis=-1)
    mixed = jnp.einsum(
        "hqk,khd->qhd",
        attn_probs.astype(jnp.bfloat16),
        heads_of(values),
        preferred_element_type=jnp.float32,
    )
    return (rows_of(mixed).astype(jnp.bfloat16), attn_probs)


def attend_back(grad_mixed, queries, keys, values, attn_probs):
    scale = HEAD_DIM ** (-0.5)
    grad_heads = heads_of(grad_mixed)
    grad_probs = jnp.einsum(
        "qhd,khd->hqk", grad_heads, heads_of(values), preferred_element_type=jnp.float32
    )
    grad_values = jnp.einsum(
        "hqk,qhd->khd",
        attn_probs.astype(jnp.bfloat16),
        grad_heads,
        preferred_element_type=jnp.float32,
    )
    grad_scores = attn_probs * (
        grad_probs - jnp.sum(attn_probs * grad_probs, axis=-1, keepdims=True)
    )
    grad_scores = grad_scores.astype(jnp.bfloat16)
    grad_queries = (
        jnp.einsum("hqk,khd->qhd", grad_scores, heads_of(keys), preferred_element_type=jnp.float32)
        * scale
    )
    grad_keys = (
        jnp.einsum(
            "hqk,qhd->khd", grad_scores, heads_of(queries), preferred_element_type=jnp.float32
        )
        * scale
    )
    return (rows_of(grad_queries), rows_of(grad_keys), rows_of(grad_values))


def segment(token_rows, memory_rows, docs, weights):
    (
        attn_gain,
        w_qkv,
        w_attn_out,
        ffn_gain,
        w_in,
        w_out,
        write_gain,
        w_write,
        w_write_out,
        init_memory,
    ) = weights
    width = token_rows.shape[1]
    seg_len = token_rows.shape[0]
    slots = memory_rows.shape[0]
    token_float = token_rows.astype(jnp.float32)
    memory_float = memory_rows.astype(jnp.float32)
    gain_attn = attn_gain.astype(jnp.float32)
    gain_ffn = ffn_gain.astype(jnp.float32)
    gain_write = write_gain.astype(jnp.float32)
    normed = norm_rows(token_float, gain_attn).astype(jnp.bfloat16)
    mem_normed = norm_rows(memory_float, gain_attn).astype(jnp.bfloat16)
    proj_all = product(normed, w_qkv).astype(jnp.bfloat16)
    mem_kv = product(mem_normed, w_qkv[:, width:]).astype(jnp.bfloat16)
    queries = proj_all[:, :width]
    keys = jnp.concatenate([mem_kv[:, :width], proj_all[:, width : 2 * width]], axis=0)
    values = jnp.concatenate([mem_kv[:, width:], proj_all[:, 2 * width :]], axis=0)
    allowed = jnp.concatenate(
        [jnp.ones((seg_len, slots), bool), docs[:, None] == docs[None, :]], axis=1
    )
    mixed, attn_probs = attend(queries, keys, values, allowed)
    hidden_one = token_float + product(mixed, w_attn_out)
    ffn_input = norm_rows(hidden_one, gain_ffn).astype(jnp.bfloat16)
    upper = product(ffn_input, w_in)
    activated = jax.nn.gelu(upper).astype(jnp.bfloat16)
    hidden_two = hidden_one + product(activated, w_out)
    write_mem = norm_rows(memory_float, gain_write).astype(jnp.bfloat16)
    write_tok = norm_rows(hidden_two, gain_write).astype(jnp.bfloat16)
    write_proj = product(write_mem, w_write).astype(jnp.bfloat16)
    write_kv = product(write_tok, w_write[:, width:]).astype(jnp.bfloat16)
    wqueries = write_proj[:, :width]
    wkeys = jnp.concatenate([write_proj[:, width : 2 * width], write_kv[:, :width]], axis=0)
    wvalues = jnp.concatenate([write_proj[:, 2 * width :], write_kv[:, width:]], axis=0)
    wallowed = jnp.concatenate(
        [jnp.eye(slots, dtype=bool), jnp.ones((slots, seg_len), bool)], axis=1
    )
    written, write_probs = attend(wqueries, wkeys, wvalues, wallowed)
    new_memory = memory_float + product(written, w_write_out)
    saved = (
        token_float,
        memory_float,
        normed,
        mem_normed,
        queries,
        keys,
        values,
        attn_probs,
        mixed,
        hidden_one,
        ffn_input,
        upper,
        activated,
        hidden_two,
        write_mem,
        write_tok,
        wqueries,
        wkeys,
        wvalues,
        write_probs,
        written,
    )
    return (hidden_two, new_memory, saved)


def segment_back(token_rows, memory_rows, docs, weights, grad_encoded, grad_memory):
    (
        attn_gain,
        w_qkv,
        w_attn_out,
        ffn_gain,
        w_in,
        w_out,
        write_gain,
        w_write,
        w_write_out,
        init_memory,
    ) = weights
    width = token_rows.shape[1]
    slots = memory_rows.shape[0]
    gain_attn = attn_gain.astype(jnp.float32)
    gain_ffn = ffn_gain.astype(jnp.float32)
    gain_write = write_gain.astype(jnp.float32)
    hidden_two, new_memory, saved = segment(token_rows, memory_rows, docs, weights)
    (
        token_float,
        memory_float,
        normed,
        mem_normed,
        queries,
        keys,
        values,
        attn_probs,
        mixed,
        hidden_one,
        ffn_input,
        upper,
        activated,
        hidden_two,
        write_mem,
        write_tok,
        wqueries,
        wkeys,
        wvalues,
        write_probs,
        written,
    ) = saved
    branch_low = grad_memory.astype(jnp.bfloat16)
    grad_write_out = product(written.T, branch_low)
    grad_written = product(branch_low, w_write_out.T).astype(jnp.bfloat16)
    grad_wq, grad_wk, grad_wv = attend_back(grad_written, wqueries, wkeys, wvalues, write_probs)
    grad_wproj = jnp.concatenate([grad_wq, grad_wk[:slots], grad_wv[:slots]], axis=1).astype(
        jnp.bfloat16
    )
    grad_wkv = jnp.concatenate([grad_wk[slots:], grad_wv[slots:]], axis=1).astype(jnp.bfloat16)
    grad_write = product(write_mem.T, grad_wproj)
    grad_write = grad_write.at[:, width:].add(product(write_tok.T, grad_wkv))
    grad_write_mem = product(grad_wproj, w_write.T)
    grad_write_tok = product(grad_wkv, w_write[:, width:].T)
    _, norm_back_mem = jax.vjp(norm_rows, memory_float, gain_write)
    grad_mem_first, grad_gain_write_one = norm_back_mem(grad_write_mem)
    _, norm_back_tok = jax.vjp(norm_rows, hidden_two, gain_write)
    grad_hidden_part, grad_gain_write_two = norm_back_tok(grad_write_tok)
    grad_hidden_two = grad_encoded + grad_hidden_part
    branch_ffn = grad_hidden_two.astype(jnp.bfloat16)
    grad_w_out = product(activated.T, branch_ffn)
    grad_activated = product(branch_ffn, w_out.T)
    _, gelu_back = jax.vjp(jax.nn.gelu, upper)
    grad_upper = gelu_back(grad_activated)[0].astype(jnp.bfloat16)
    grad_w_in = product(ffn_input.T, grad_upper)
    grad_ffn_input = product(grad_upper, w_in.T)
    _, norm_back_ffn = jax.vjp(norm_rows, hidden_one, gain_ffn)
    grad_hidden_ffn, grad_gain_ffn = norm_back_ffn(grad_ffn_input)
    grad_hidden_one = grad_hidden_two + grad_hidden_ffn
    branch_attn = grad_hidden_one.astype(jnp.bfloat16)
    grad_attn_out = product(mixed.T, branch_attn)
    grad_mixed = product(branch_attn, w_attn_out.T).astype(jnp.bfloat16)
    grad_q, grad_k, grad_v = attend_back(grad_mixed, queries, keys, values, attn_probs)
    grad_proj = jnp.concatenate([grad_q, grad_k[slots:], grad_v[slots:]], axis=1).astype(
        jnp.bfloat16
    )
    grad_mem_kv = jnp.concatenate([grad_k[:slots], grad_v[:slots]], axis=1).astype(jnp.bfloat16)
    grad_qkv = product(normed.T, grad_proj)
    grad_qkv = grad_qkv.at[:, width:].add(product(mem_normed.T, grad_mem_kv))
    grad_normed = product(grad_proj, w_qkv.T)
    grad_mem_normed = product(grad_mem_kv, w_qkv[:, width:].T)
    _, norm_back_tokens = jax.vjp(norm_rows, token_float, gain_attn)
    grad_token_part, grad_gain_attn_one = norm_back_tokens(grad_normed)
    _, norm_back_memory = jax.vjp(norm_rows, memory_float, gain_attn)
    grad_mem_second, grad_gain_attn_two = norm_back_memory(grad_mem_normed)
    grad_tokens = grad_hidden_one + grad_token_part
    grad_memory_in = grad_memory + grad_mem_first + grad_mem_second
    weight_grads = (
        grad_gain_attn_one + grad_gain_attn_two,
        grad_qkv,
        grad_attn_out,
        grad_gain_ffn,
        grad_w_in,
        grad_w_out,
        grad_gain_write_one + grad_gain_write_two,
        grad_write,
        grad_write_out,
    )
    return (grad_tokens, weight_grads, grad_memory_in)


def put_row(buffer, row, index):
    return lax.dynamic_update_index_in_dim(buffer, row, index, 0)


def body(
    tokens,
    doc_ids,
    reset_flags,
    attn_gain,
    w_qkv,
    w_attn_out,
    ffn_gain,
    w_in,
    w_out,
    write_gain,
    w_write,
    w_write_out,
    init_memory,
    out_grad,
    memory_grad,
):
    weights = (
        attn_gain,
        w_qkv,
        w_attn_out,
        ffn_gain,
        w_in,
        w_out,
        write_gain,
        w_write,
        w_write_out,
        init_memory,
    )
    micro = tokens.shape[0]
    seg_len = tokens.shape[2]
    width = tokens.shape[3]
    slots = init_memory.shape[0]
    sections = lax.axis_size("section")
    place = lax.axis_index("section")

    def plan(step, backward):
        level = sections - 1 - place if backward else place
        micro_index = step // sections
        active_now = step % sections == level
        clipped = jnp.clip(micro_index, 0, micro - 1).astype(jnp.int32)
        target = jnp.where(active_now, clipped, micro)
        return (clipped, target, active_now)

    def sweep(step_fn, carry):
        for block in range(micro):
            carry = lax.fori_loop(block * sections, (block + 1) * sections, step_fn, carry)
        return carry

    def forward_step(step, carry):
        arriving, kept, outputs, written_all = carry
        micro_index, target, active_now = plan(step, False)
        start = jnp.where(reset_flags[micro_index, 0] > 0, init_memory, arriving)

        def forward_compute(unused):
            hidden_two, new_memory, saved = segment(
                tokens[micro_index, 0], start, doc_ids[micro_index, 0], weights
            )
            return (hidden_two.astype(jnp.bfloat16), new_memory.astype(jnp.bfloat16))

        def forward_skip(unused):
            return (
                jnp.zeros((seg_len, width), jnp.bfloat16),
                jnp.zeros((slots, width), jnp.bfloat16),
            )

        encoded_now, written_now = lax.cond(active_now, forward_compute, forward_skip, None)
        kept = put_row(kept, start, target)
        outputs = put_row(outputs, encoded_now, target)
        written_all = put_row(written_all, written_now, target)
        arriving = shifted(written_now, "section", 1)
        return (arriving, kept, outputs, written_all)

    forward_init = (
        jnp.zeros((slots, width), jnp.bfloat16),
        jnp.zeros((micro + 1, slots, width), jnp.bfloat16),
        jnp.zeros((micro + 1, seg_len, width), jnp.bfloat16),
        jnp.zeros((micro + 1, slots, width), jnp.bfloat16),
    )
    arriving, kept, outputs, written_all = sweep(forward_step, forward_init)

    def backward_step(step, carry):
        returning, grads, token_grads = carry
        micro_index, target, active_now = plan(step, True)
        reset_now = reset_flags[micro_index, 0] > 0

        def backward_compute(unused):
            memory_cot = memory_grad[micro_index, 0].astype(jnp.float32) + returning.astype(
                jnp.float32
            )
            grad_tokens, weight_grads, grad_memory_in = segment_back(
                tokens[micro_index, 0],
                kept[micro_index],
                doc_ids[micro_index, 0],
                weights,
                out_grad[micro_index, 0].astype(jnp.float32),
                memory_cot,
            )
            init_part = jnp.where(reset_now, grad_memory_in, 0.0)
            sending = jnp.where(reset_now, 0.0, grad_memory_in).astype(jnp.bfloat16)
            return (grad_tokens, weight_grads + (init_part,), sending)

        def backward_skip(unused):
            return (
                jnp.zeros((seg_len, width), jnp.float32),
                tuple((jnp.zeros(w.shape, jnp.float32) for w in weights)),
                jnp.zeros((slots, width), jnp.bfloat16),
            )

        grad_tokens, weight_grads, sending = lax.cond(
            active_now, backward_compute, backward_skip, None
        )
        grads = tuple((a + b for a, b in zip(grads, weight_grads)))
        token_grads = put_row(token_grads, grad_tokens, target)
        returning = shifted(sending, "section", -1)
        return (returning, grads, token_grads)

    backward_init = (
        jnp.zeros((slots, width), jnp.bfloat16),
        tuple((jnp.zeros(w.shape, jnp.float32) for w in weights)),
        jnp.zeros((micro + 1, seg_len, width), jnp.float32),
    )
    returning, grads, token_grads = sweep(backward_step, backward_init)
    (
        grad_attn_gain,
        grad_qkv_w,
        grad_attn_out,
        grad_ffn_gain,
        grad_in_w,
        grad_out_w,
        grad_write_gain,
        grad_write_w,
        grad_write_out,
        grad_init,
    ) = grads
    totals = lax.psum(
        (
            grad_attn_gain,
            grad_qkv_w,
            grad_attn_out,
            grad_ffn_gain,
            grad_in_w,
            grad_out_w,
            grad_write_gain,
            grad_write_w,
            grad_write_out,
            grad_init,
        ),
        ("section", "dp"),
    )
    return (
        outputs[:micro, None],
        written_all[:micro, None],
        token_grads[:micro, None],
        totals[0],
        totals[1],
        totals[2],
        totals[3],
        totals[4],
        totals[5],
        totals[6],
        totals[7],
        totals[8],
        totals[9],
    )


def solution(mesh):
    placed = (
        P("dp", "section", None, None),
        P("dp", "section", None),
        P("dp", "section"),
        P(),
        P(),
        P(),
        P(),
        P(),
        P(),
        P(),
        P(),
        P(),
        P(),
        P("dp", "section", None, None),
        P("dp", "section", None, None),
    )
    return jax.shard_map(
        body,
        mesh=mesh,
        in_specs=placed,
        out_specs=(
            P("dp", "section", None, None),
            P("dp", "section", None, None),
            P("dp", "section", None, None),
            P(),
            P(),
            P(),
            P(),
            P(),
            P(),
            P(),
            P(),
            P(),
            P(),
        ),
        check_vma=False,
    )
```

profile of v0, /device:TPU:0, one launch (start us, length us, event | category | flops | bytes accessed | tf_op | source)
XLA Modules:
  0.0 3328.1 jit_solution(17256782917369843282)
XLA Ops:
  18.3 215.7 %while.241 = (s32[]{:T(128)}, bf16[64,512]{1,0:T(8,128)(2,1)S(1)}, bf16[5,64,512]{2,1,0:T(8,128)(2,1)S(1)}, bf16[5,512,512]{1,2,0:T(8,128)(2,1)}, bf16[5,64,512]...) while((s32[]{:T(128)}, bf16[64,512]{1,0:T(8,128)(2,1)S(1)}, ...), condition=%wide.region_11.12_spmd, body=%wide.region_0.11_spmd.sunk | while | flops 4677017600 | bytes 67435600 | solution.py:309
  21.7 60.9 %conditional.17 = (bf16[64,512]{1,0:T(8,128)(2,1)}, bf16[1,64,512]{2,1,0:T(8,128)(2,1)S(1)}, bf16[1,512,512]{1,2,0:T(8,128)(2,1)S(1)}) conditional(s32[]{:T(128)} %convert_element_type.1521, () %tuple.587, (bf16[64,512]{1,0:T(8,128)(2,1)}, bf16[512]{0:T(512)(128)(2,1)S(1)}, bf16[512,1536]{1,0:T(8,128)(2,1)S(1)}, s32[]{:T(128)}, ...), branch_computations={%region_1.1_spmd, %region_2.10_spmd} | conditional | flops 4676984832 | bytes 65468944 | solution.py:329
  41.8 8.4 fusion.756
  91.6 61.3 %collective-permute-start = (bf16[64,512]{1,0:T(8,128)(2,1)}, bf16[64,512]{1,0:T(8,128)(2,1)S(1)}, u32[]{:S(2)}, u32[]{:S(2)}) collective-permute-start(bf16[64,512]{1,0:T(8,128)(2,1)} %get-tuple-element.7501), channel_id=1, source_target_pairs={{0,8},{8,16},{16,24},{1,9},{9,17},{17,25},{2,10},{10,18},{18,26},{... | collective-permute-start | bytes 196616 | tf_op jit(solution)/shard_map/while/body/eval_jaxpr/ppermute | solution.py:17
  168.8 62.9 %collective-permute-start = (bf16[64,512]{1,0:T(8,128)(2,1)}, bf16[64,512]{1,0:T(8,128)(2,1)S(1)}, u32[]{:S(2)}, u32[]{:S(2)}) collective-permute-start(bf16[64,512]{1,0:T(8,128)(2,1)} %get-tuple-element.7501), channel_id=1, source_target_pairs={{0,8},{8,16},{16,24},{1,9},{9,17},{17,25},{2,10},{10,18},{18,26},{... | collective-permute-start | bytes 196616 | tf_op jit(solution)/shard_map/while/body/eval_jaxpr/ppermute | solution.py:17
  234.1 214.4 %while.242 = (s32[]{:T(128)}, bf16[64,512]{1,0:T(8,128)(2,1)S(1)}, bf16[5,64,512]{2,1,0:T(8,128)(2,1)S(1)}, bf16[5,512,512]{1,2,0:T(8,128)(2,1)}, bf16[5,64,512]...) while((s32[]{:T(128)}, bf16[64,512]{1,0:T(8,128)(2,1)S(1)}, ...), condition=%wide.region_23.24_spmd, body=%wide.region_12.23_spmd.sunk | while | flops 4677017600 | bytes 67435696 | solution.py:309
  237.8 60.9 %conditional.18 = (bf16[64,512]{1,0:T(8,128)(2,1)}, bf16[1,64,512]{2,1,0:T(8,128)(2,1)S(1)}, bf16[1,512,512]{1,2,0:T(8,128)(2,1)S(1)}) conditional(s32[]{:T(128)} %convert_element_type.1522, () %tuple.591, (bf16[64,512]{1,0:T(8,128)(2,1)}, bf16[512]{0:T(512)(128)(2,1)S(1)}, bf16[512,1536]{1,0:T(8,128)(2,1)S(1)}, s32[]{:T(128)}, ...), branch_computations={%region_13.13_spmd, %region_14.22_spmd} | conditional | flops 4676984832 | bytes 65468944 | solution.py:329
  257.8 8.4 fusion.764
  307.7 60.4 %collective-permute-start.1 = (bf16[64,512]{1,0:T(8,128)(2,1)}, bf16[64,512]{1,0:T(8,128)(2,1)S(1)}, u32[]{:S(2)}, u32[]{:S(2)}) collective-permute-start(bf16[64,512]{1,0:T(8,128)(2,1)} %get-tuple-element.7525), channel_id=1, source_target_pairs={{0,8},{8,16},{16,24},{1,9},{9,17},{17,25},{2,10},{10,18},{18,26},{... | collective-permute-start | bytes 196616 | tf_op jit(solution)/shard_map/while/body/eval_jaxpr/ppermute | solution.py:17
  383.5 62.6 %collective-permute-start.1 = (bf16[64,512]{1,0:T(8,128)(2,1)}, bf16[64,512]{1,0:T(8,128)(2,1)S(1)}, u32[]{:S(2)}, u32[]{:S(2)}) collective-permute-start(bf16[64,512]{1,0:T(8,128)(2,1)} %get-tuple-element.7525), channel_id=1, source_target_pairs={{0,8},{8,16},{16,24},{1,9},{9,17},{17,25},{2,10},{10,18},{18,26},{... | collective-permute-start | bytes 196616 | tf_op jit(solution)/shard_map/while/body/eval_jaxpr/ppermute | solution.py:17
  448.5 216.5 %while.243 = (s32[]{:T(128)}, bf16[64,512]{1,0:T(8,128)(2,1)S(1)}, bf16[5,64,512]{2,1,0:T(8,128)(2,1)S(1)}, bf16[5,512,512]{1,2,0:T(8,128)(2,1)}, bf16[5,64,512]...) while((s32[]{:T(128)}, bf16[64,512]{1,0:T(8,128)(2,1)S(1)}, ...), condition=%wide.region_35.36_spmd, body=%wide.region_24.35_spmd.sunk | while | flops 4677017600 | bytes 67435704 | solution.py:309
  452.0 60.9 %conditional.19 = (bf16[64,512]{1,0:T(8,128)(2,1)}, bf16[1,64,512]{2,1,0:T(8,128)(2,1)S(1)}, bf16[1,512,512]{1,2,0:T(8,128)(2,1)S(1)}) conditional(s32[]{:T(128)} %convert_element_type.1523, () %tuple.595, (bf16[64,512]{1,0:T(8,128)(2,1)}, bf16[512]{0:T(512)(128)(2,1)S(1)}, bf16[512,1536]{1,0:T(8,128)(2,1)S(1)}, s32[]{:T(128)}, ...), branch_computations={%region_25.25_spmd, %region_26.34_spmd} | conditional | flops 4676984832 | bytes 65468944 | solution.py:329
  472.1 8.4 fusion.772
  521.9 61.9 %collective-permute-start.2 = (bf16[64,512]{1,0:T(8,128)(2,1)}, bf16[64,512]{1,0:T(8,128)(2,1)S(1)}, u32[]{:S(2)}, u32[]{:S(2)}) collective-permute-start(bf16[64,512]{1,0:T(8,128)(2,1)} %get-tuple-element.7549), channel_id=1, source_target_pairs={{0,8},{8,16},{16,24},{1,9},{9,17},{17,25},{2,10},{10,18},{18,26},{... | collective-permute-start | bytes 196616 | tf_op jit(solution)/shard_map/while/body/eval_jaxpr/ppermute | solution.py:17
  599.8 62.9 %collective-permute-start.2 = (bf16[64,512]{1,0:T(8,128)(2,1)}, bf16[64,512]{1,0:T(8,128)(2,1)S(1)}, u32[]{:S(2)}, u32[]{:S(2)}) collective-permute-start(bf16[64,512]{1,0:T(8,128)(2,1)} %get-tuple-element.7549), channel_id=1, source_target_pairs={{0,8},{8,16},{16,24},{1,9},{9,17},{17,25},{2,10},{10,18},{18,26},{... | collective-permute-start | bytes 196616 | tf_op jit(solution)/shard_map/while/body/eval_jaxpr/ppermute | solution.py:17
  665.0 214.5 %while.244 = (s32[]{:T(128)}, bf16[64,512]{1,0:T(8,128)(2,1)S(1)}, bf16[5,64,512]{2,1,0:T(8,128)(2,1)S(1)}, bf16[5,512,512]{1,2,0:T(8,128)(2,1)}, bf16[5,64,512]...) while((s32[]{:T(128)}, bf16[64,512]{1,0:T(8,128)(2,1)S(1)}, ...), condition=%wide.region_47.48_spmd, body=%wide.region_36.47_spmd.sunk | while | flops 4677017600 | bytes 67435704 | solution.py:309
  668.8 60.9 %conditional.20 = (bf16[64,512]{1,0:T(8,128)(2,1)}, bf16[1,64,512]{2,1,0:T(8,128)(2,1)S(1)}, bf16[1,512,512]{1,2,0:T(8,128)(2,1)S(1)}) conditional(s32[]{:T(128)} %convert_element_type.1524, () %tuple.599, (bf16[64,512]{1,0:T(8,128)(2,1)}, bf16[512]{0:T(512)(128)(2,1)S(1)}, bf16[512,1536]{1,0:T(8,128)(2,1)S(1)}, s32[]{:T(128)}, ...), branch_computations={%region_37.37_spmd, %region_38.46_spmd} | conditional | flops 4676984832 | bytes 65468944 | solution.py:329
  688.8 8.4 fusion.780
  738.7 60.4 %collective-permute-start.3 = (bf16[64,512]{1,0:T(8,128)(2,1)}, bf16[64,512]{1,0:T(8,128)(2,1)S(1)}, u32[]{:S(2)}, u32[]{:S(2)}) collective-permute-start(bf16[64,512]{1,0:T(8,128)(2,1)} %get-tuple-element.7573), channel_id=1, source_target_pairs={{0,8},{8,16},{16,24},{1,9},{9,17},{17,25},{2,10},{10,18},{18,26},{... | collective-permute-start | bytes 196616 | tf_op jit(solution)/shard_map/while/body/eval_jaxpr/ppermute | solution.py:17
  814.5 62.6 %collective-permute-start.3 = (bf16[64,512]{1,0:T(8,128)(2,1)}, bf16[64,512]{1,0:T(8,128)(2,1)S(1)}, u32[]{:S(2)}, u32[]{:S(2)}) collective-permute-start(bf16[64,512]{1,0:T(8,128)(2,1)} %get-tuple-element.7573), channel_id=1, source_target_pairs={{0,8},{8,16},{16,24},{1,9},{9,17},{17,25},{2,10},{10,18},{18,26},{... | collective-permute-start | bytes 196616 | tf_op jit(solution)/shard_map/while/body/eval_jaxpr/ppermute | solution.py:17
  882.5 621.9 %while.248 = (s32[]{:T(128)}, bf16[64,512]{1,0:T(8,128)(2,1)S(1)}, f32[512]{0:T(512)}, f32[512,1536]{1,0:T(8,128)}, f32[512,512]{1,0:T(8,128)}, /*index=5*/f32[5...) while((s32[]{:T(128)}, bf16[64,512]{1,0:T(8,128)(2,1)S(1)}, ...), condition=%wide.region_71.72_spmd.clone, body=%wide.region_48.71_spmd.clone.sunk | while | flops 14018064384 | bytes 486583296 | solution.py:309
  883.3 17.7 conditional.24
  926.6 13.9 conditional.24
  961.9 8.9 select_add_fusion.18
  971.8 11.9 collective-permute-done.7
  984.4 13.9 conditional.24
  1019.7 8.9 select_add_fusion.18
  1029.7 312.8 %collective-permute-done.7 = bf16[64,512]{1,0:T(8,128)(2,1)S(1)} collective-permute-done((bf16[64,512]{1,0:T(8,128)(2,1)}, bf16[64,512]{1,0:T(8,128)(2,1)S(1)}, u32[]{:S(2)}, u32[]{:S(2)}) %collective-permute-start.7) | collective-permute-done | bytes 65568 | tf_op jit(solution)/shard_map/while/body/eval_jaxpr/ppermute | solution.py:17
  1343.1 129.0 %conditional.24 = (f32[512]{0:T(512)S(1)}, f32[512,1536]{1,0:T(8,128)}, f32[512,512]{1,0:T(8,128)S(1)}, f32[512]{0:T(512)}, f32[512,2048]{1,0:T(8,128)}, /*index...) conditional(s32[]{:T(128)} %convert_element_type.1528, ...), branch_computations={%region_49.49_spmd, %region_50.70_spmd} | conditional | flops 14009607168 | bytes 416636896 | solution.py:372
  1366.1 9.0 fusion.792
  1442.0 11.2 multiply_convert_fusion.32
  1493.4 8.9 select_add_fusion.18
  1504.4 502.4 %while.245 = (s32[]{:T(128)}, bf16[64,512]{1,0:T(8,128)(2,1)S(1)}, f32[512]{0:T(512)}, f32[512,1536]{1,0:T(8,128)}, f32[512,512]{1,0:T(8,128)}, /*index=5*/f32[5...) while((s32[]{:T(128)}, bf16[64,512]{1,0:T(8,128)(2,1)S(1)}, ...), condition=%wide.region_95.96_spmd, body=%wide.region_72.95_spmd.sunk | while | flops 14013835264 | bytes 511716320 | solution.py:309
  1512.6 17.0 conditional.21
  1558.5 8.0 add.2082
  1567.3 13.4 conditional.21
  1609.5 8.0 add.2082
  1618.3 13.4 conditional.21
  1668.5 170.9 %collective-permute-done.4 = bf16[64,512]{1,0:T(8,128)(2,1)S(1)} collective-permute-done((bf16[64,512]{1,0:T(8,128)(2,1)}, bf16[64,512]{1,0:T(8,128)(2,1)S(1)}, u32[]{:S(2)}, u32[]{:S(2)}) %collective-permute-start.4) | collective-permute-done | bytes 65568 | tf_op jit(solution)/shard_map/while/body/eval_jaxpr/ppermute | solution.py:17
  1840.0 129.0 %conditional.21 = (f32[512]{0:T(512)S(1)}, f32[512,1536]{1,0:T(8,128)}, f32[512,512]{1,0:T(8,128)S(1)}, f32[512]{0:T(512)}, f32[512,2048]{1,0:T(8,128)}, /*index...) conditional(s32[]{:T(128)} %convert_element_type.1525, ...), branch_computations={%region_73.73_spmd, %region_74.94_spmd} | conditional | flops 14009607168 | bytes 416645120 | solution.py:372
  1863.1 9.0 fusion.799
  1938.9 11.2 multiply_convert_fusion.43
  2006.9 503.0 %while.246 = (s32[]{:T(128)}, bf16[64,512]{1,0:T(8,128)(2,1)S(1)}, f32[512]{0:T(512)}, f32[512,1536]{1,0:T(8,128)}, f32[512,512]{1,0:T(8,128)}, /*index=5*/f32[5...) while((s32[]{:T(128)}, bf16[64,512]{1,0:T(8,128)(2,1)S(1)}, ...), condition=%wide.region_119.120_spmd, body=%wide.region_96.119_spmd.sunk | while | flops 14013835264 | bytes 511716320 | solution.py:309
  2015.0 17.0 conditional.22
  2060.9 8.0 add.2095
  2069.7 13.4 conditional.22
  2111.9 8.0 add.2095
  2120.7 13.4 conditional.22
  2162.9 8.0 add.2095
  2170.9 171.3 %collective-permute-done.5 = bf16[64,512]{1,0:T(8,128)(2,1)S(1)} collective-permute-done((bf16[64,512]{1,0:T(8,128)(2,1)}, bf16[64,512]{1,0:T(8,128)(2,1)S(1)}, u32[]{:S(2)}, u32[]{:S(2)}) %collective-permute-start.5) | collective-permute-done | bytes 65568 | tf_op jit(solution)/shard_map/while/body/eval_jaxpr/ppermute | solution.py:17
  2342.8 129.2 %conditional.22 = (f32[512]{0:T(512)S(1)}, f32[512,1536]{1,0:T(8,128)}, f32[512,512]{1,0:T(8,128)S(1)}, f32[512]{0:T(512)}, f32[512,2048]{1,0:T(8,128)}, /*index...) conditional(s32[]{:T(128)} %convert_element_type.1526, ...), branch_computations={%region_97.97_spmd, %region_98.118_spmd} | conditional | flops 14009607168 | bytes 416645120 | solution.py:372
  2365.9 9.0 fusion.806
  2441.8 11.2 multiply_convert_fusion.54
  2500.8 8.0 add.2095
  2509.9 504.2 %while.247 = (s32[]{:T(128)}, bf16[64,512]{1,0:T(8,128)(2,1)S(1)}, f32[512]{0:T(512)}, f32[512,1536]{1,0:T(8,128)}, f32[512,512]{1,0:T(8,128)}, /*index=5*/f32[5...) while((s32[]{:T(128)}, bf16[64,512]{1,0:T(8,128)(2,1)S(1)}, ...), condition=%wide.region_143.144_spmd, body=%wide.region_120.143_spmd.sunk | while | flops 14013835264 | bytes 511716320 | solution.py:309
  2518.0 17.0 conditional.23
  2572.7 13.4 conditional.23
  2623.7 13.4 conditional.23
  2673.9 171.1 %collective-permute-done.6 = bf16[64,512]{1,0:T(8,128)(2,1)S(1)} collective-permute-done((bf16[64,512]{1,0:T(8,128)(2,1)}, bf16[64,512]{1,0:T(8,128)(2,1)S(1)}, u32[]{:S(2)}, u32[]{:S(2)}) %collective-permute-start.6) | collective-permute-done | bytes 65568 | tf_op jit(solution)/shard_map/while/body/eval_jaxpr/ppermute | solution.py:17
  2845.6 129.1 %conditional.23 = (f32[512]{0:T(512)S(1)}, f32[512,1536]{1,0:T(8,128)}, f32[512,512]{1,0:T(8,128)S(1)}, f32[512]{0:T(512)}, f32[512,2048]{1,0:T(8,128)}, /*index...) conditional(s32[]{:T(128)} %convert_element_type.1527, ...), branch_computations={%region_121.121_spmd, %region_122.142_spmd} | conditional | flops 14009607168 | bytes 416645120 | solution.py:372
  2868.8 9.0 fusion.813
  2944.6 11.2 multiply_convert_fusion.65
  3025.6 44.3 %all-reduce.16 = (f32[512]{0:T(512)}, f32[512]{0:T(512)}, f32[512]{0:T(512)}) all-reduce(f32[512]{0:T(512)S(1)} %copy-done.177, f32[512]{0:T(512)S(1)} %copy-done.176, f32[512]{0:T(512)S(1)} %copy-done.173), channel_id=1, replica_groups=mesh['section'=4,'dp'=8] {'section','dp'}, use_global_device_ids=true, to_apply=%region_144.145 | all-reduce | flops 1536 | bytes 12288 | tf_op jit(solution)/shard_map/psum | solution.py:398
  3078.6 226.6 %all-reduce.20.cloned.1.call-done = (f32[512,1536]{1,0:T(8,128)}, f32[512,512]{1,0:T(8,128)}, f32[512,2048]{1,0:T(8,128)}, f32[2048,512]{1,0:T(8,128)}, f32[512,...) async-done(((f32[512,1536]{1,0:T(8,128)}, f32[512,512]{1,0:T(8,128)}, f32[512,2048]{1,0:T(8,128)}, f32[2048,512]{1,0:T(8,128)}, f32[512,1536]{1,0:T(8,128)}, ...) | async-done | bytes 16908304 | tf_op jit(solution)/shard_map/psum | solution.py:398
  (1858 shorter events, 1475.6 us)
Async XLA Ops:
  7.2 3298.0 %all-reduce.20.cloned.1.call-start = ((), (), s32[]{:S(2)}) async-start(), calls=%async_computation | async-start | bytes 33816576 | tf_op jit(solution)/shard_map/psum | solution.py:398
  57.7 8.6 copy-start.219
  83.3 3.6 collective-permute-start
  91.6 63.6 %collective-permute-start = (bf16[64,512]{1,0:T(8,128)(2,1)}, bf16[64,512]{1,0:T(8,128)(2,1)S(1)}, u32[]{:S(2)}, u32[]{:S(2)}) collective-permute-start(bf16[64,512]{1,0:T(8,128)(2,1)} %get-tuple-element.7501), channel_id=1, source_target_pairs={{0,8},{8,16},{16,24},{1,9},{9,17},{17,25},{2,10},{10,18},{18,26},{... | collective-permute-start | bytes 196616 | tf_op jit(solution)/shard_map/while/body/eval_jaxpr/ppermute | solution.py:17
  159.9 4.2 collective-permute-start
  168.8 65.2 %collective-permute-start = (bf16[64,512]{1,0:T(8,128)(2,1)}, bf16[64,512]{1,0:T(8,128)(2,1)S(1)}, u32[]{:S(2)}, u32[]{:S(2)}) collective-permute-start(bf16[64,512]{1,0:T(8,128)(2,1)} %get-tuple-element.7501), channel_id=1, source_target_pairs={{0,8},{8,16},{16,24},{1,9},{9,17},{17,25},{2,10},{10,18},{18,26},{... | collective-permute-start | bytes 196616 | tf_op jit(solution)/shard_map/while/body/eval_jaxpr/ppermute | solution.py:17
  273.7 8.6 copy-start.221
  299.4 3.6 collective-permute-start.1
  307.7 62.8 %collective-permute-start.1 = (bf16[64,512]{1,0:T(8,128)(2,1)}, bf16[64,512]{1,0:T(8,128)(2,1)S(1)}, u32[]{:S(2)}, u32[]{:S(2)}) collective-permute-start(bf16[64,512]{1,0:T(8,128)(2,1)} %get-tuple-element.7525), channel_id=1, source_target_pairs={{0,8},{8,16},{16,24},{1,9},{9,17},{17,25},{2,10},{10,18},{18,26},{... | collective-permute-start | bytes 196616 | tf_op jit(solution)/shard_map/while/body/eval_jaxpr/ppermute | solution.py:17
  375.2 3.6 collective-permute-start.1
  383.5 65.0 %collective-permute-start.1 = (bf16[64,512]{1,0:T(8,128)(2,1)}, bf16[64,512]{1,0:T(8,128)(2,1)S(1)}, u32[]{:S(2)}, u32[]{:S(2)}) collective-permute-start(bf16[64,512]{1,0:T(8,128)(2,1)} %get-tuple-element.7525), channel_id=1, source_target_pairs={{0,8},{8,16},{16,24},{1,9},{9,17},{17,25},{2,10},{10,18},{18,26},{... | collective-permute-start | bytes 196616 | tf_op jit(solution)/shard_map/while/body/eval_jaxpr/ppermute | solution.py:17
  488.0 8.6 copy-start.223
  513.6 3.6 collective-permute-start.2
  521.9 64.3 %collective-permute-start.2 = (bf16[64,512]{1,0:T(8,128)(2,1)}, bf16[64,512]{1,0:T(8,128)(2,1)S(1)}, u32[]{:S(2)}, u32[]{:S(2)}) collective-permute-start(bf16[64,512]{1,0:T(8,128)(2,1)} %get-tuple-element.7549), channel_id=1, source_target_pairs={{0,8},{8,16},{16,24},{1,9},{9,17},{17,25},{2,10},{10,18},{18,26},{... | collective-permute-start | bytes 196616 | tf_op jit(solution)/shard_map/while/body/eval_jaxpr/ppermute | solution.py:17
  590.9 4.2 collective-permute-start.2
  599.8 65.2 %collective-permute-start.2 = (bf16[64,512]{1,0:T(8,128)(2,1)}, bf16[64,512]{1,0:T(8,128)(2,1)S(1)}, u32[]{:S(2)}, u32[]{:S(2)}) collective-permute-start(bf16[64,512]{1,0:T(8,128)(2,1)} %get-tuple-element.7549), channel_id=1, source_target_pairs={{0,8},{8,16},{16,24},{1,9},{9,17},{17,25},{2,10},{10,18},{18,26},{... | collective-permute-start | bytes 196616 | tf_op jit(solution)/shard_map/while/body/eval_jaxpr/ppermute | solution.py:17
  704.7 8.6 copy-start.225
  730.4 3.6 collective-permute-start.3
  738.7 62.8 %collective-permute-start.3 = (bf16[64,512]{1,0:T(8,128)(2,1)}, bf16[64,512]{1,0:T(8,128)(2,1)S(1)}, u32[]{:S(2)}, u32[]{:S(2)}) collective-permute-start(bf16[64,512]{1,0:T(8,128)(2,1)} %get-tuple-element.7573), channel_id=1, source_target_pairs={{0,8},{8,16},{16,24},{1,9},{9,17},{17,25},{2,10},{10,18},{18,26},{... | collective-permute-start | bytes 196616 | tf_op jit(solution)/shard_map/while/body/eval_jaxpr/ppermute | solution.py:17
  806.2 3.6 collective-permute-start.3
  814.5 65.0 %collective-permute-start.3 = (bf16[64,512]{1,0:T(8,128)(2,1)}, bf16[64,512]{1,0:T(8,128)(2,1)S(1)}, u32[]{:S(2)}, u32[]{:S(2)}) collective-permute-start(bf16[64,512]{1,0:T(8,128)(2,1)} %get-tuple-element.7573), channel_id=1, source_target_pairs={{0,8},{8,16},{16,24},{1,9},{9,17},{17,25},{2,10},{10,18},{18,26},{... | collective-permute-start | bytes 196616 | tf_op jit(solution)/shard_map/while/body/eval_jaxpr/ppermute | solution.py:17
  902.0 23.8 collective-permute-start.7
  917.6 8.2 copy-start.152
  917.6 8.2 copy-start.161
  941.5 42.3 %collective-permute-start.7 = (bf16[64,512]{1,0:T(8,128)(2,1)}, bf16[64,512]{1,0:T(8,128)(2,1)S(1)}, u32[]{:S(2)}, u32[]{:S(2)}) collective-permute-start(bf16[64,512]{1,0:T(8,128)(2,1)} %get-tuple-element.7729), channel_id=1, source_target_pairs={{8,0},{16,8},{24,16},{9,1},{17,9},{25,17},{10,2},{18,10},{26,18},{... | collective-permute-start | bytes 196616 | tf_op jit(solution)/shard_map/while/body/eval_jaxpr/ppermute | solution.py:17
  961.8 8.9 copy-start.62
  961.8 21.9 copy-start.152
  961.8 21.9 copy-start.161
  999.3 343.1 %collective-permute-start.7 = (bf16[64,512]{1,0:T(8,128)(2,1)}, bf16[64,512]{1,0:T(8,128)(2,1)S(1)}, u32[]{:S(2)}, u32[]{:S(2)}) collective-permute-start(bf16[64,512]{1,0:T(8,128)(2,1)} %get-tuple-element.7729), channel_id=1, source_target_pairs={{8,0},{16,8},{24,16},{9,1},{17,9},{25,17},{10,2},{18,10},{26,18},{... | collective-permute-start | bytes 196616 | tf_op jit(solution)/shard_map/while/body/eval_jaxpr/ppermute | solution.py:17
  1019.6 8.9 copy-start.62
  1019.7 322.8 %copy-start.152 = (bf16[512]{0:T(512)(128)(2,1)S(1)}, bf16[512]{0:T(512)(128)(2,1)}, u32[]{:S(2)}) copy-start(bf16[512]{0:T(512)(128)(2,1)} %copy-done.151) | copy-start | bytes 3076 | tf_op jit(solution)/shard_map/while
  1019.7 322.8 %copy-start.161 = (bf16[512]{0:T(512)(128)(2,1)S(1)}, bf16[512]{0:T(512)(128)(2,1)}, u32[]{:S(2)}) copy-start(bf16[512]{0:T(512)(128)(2,1)} %copy-done.160) | copy-start | bytes 3076 | tf_op jit(solution)/shard_map/while
  1345.0 8.2 copy-start.242
  1415.3 9.1 slice-start
  1415.3 9.1 slice-start.1
  1473.1 30.3 collective-permute-start.7
  1493.4 8.9 copy-start.62
  1493.4 9.9 copy-start.152
  1493.4 9.9 copy-start.161
  1531.2 35.2 %collective-permute-start.4 = (bf16[64,512]{1,0:T(8,128)(2,1)}, bf16[64,512]{1,0:T(8,128)(2,1)S(1)}, u32[]{:S(2)}, u32[]{:S(2)}) collective-permute-start(bf16[64,512]{1,0:T(8,128)(2,1)} %get-tuple-element.7606), channel_id=1, source_target_pairs={{8,0},{16,8},{24,16},{9,1},{17,9},{25,17},{10,2},{18,10},{26,18},{... | collective-permute-start | bytes 196616 | tf_op jit(solution)/shard_map/while/body/eval_jaxpr/ppermute | solution.py:17
  1582.3 35.2 %collective-permute-start.4 = (bf16[64,512]{1,0:T(8,128)(2,1)}, bf16[64,512]{1,0:T(8,128)(2,1)S(1)}, u32[]{:S(2)}, u32[]{:S(2)}) collective-permute-start(bf16[64,512]{1,0:T(8,128)(2,1)} %get-tuple-element.7606), channel_id=1, source_target_pairs={{8,0},{16,8},{24,16},{9,1},{17,9},{25,17},{10,2},{18,10},{26,18},{... | collective-permute-start | bytes 196616 | tf_op jit(solution)/shard_map/while/body/eval_jaxpr/ppermute | solution.py:17
  1633.2 206.1 %collective-permute-start.4 = (bf16[64,512]{1,0:T(8,128)(2,1)}, bf16[64,512]{1,0:T(8,128)(2,1)S(1)}, u32[]{:S(2)}, u32[]{:S(2)}) collective-permute-start(bf16[64,512]{1,0:T(8,128)(2,1)} %get-tuple-element.7606), channel_id=1, source_target_pairs={{8,0},{16,8},{24,16},{9,1},{17,9},{25,17},{10,2},{18,10},{26,18},{... | collective-permute-start | bytes 196616 | tf_op jit(solution)/shard_map/while/body/eval_jaxpr/ppermute | solution.py:17
  1660.4 178.9 %copy-start.154 = (bf16[512]{0:T(512)(128)(2,1)S(1)}, bf16[512]{0:T(512)(128)(2,1)}, u32[]{:S(2)}) copy-start(bf16[512]{0:T(512)(128)(2,1)} %copy-done.153) | copy-start | bytes 3076 | tf_op jit(solution)/shard_map/while
  1660.5 178.9 %copy-start.163 = (bf16[512]{0:T(512)(128)(2,1)S(1)}, bf16[512]{0:T(512)(128)(2,1)}, u32[]{:S(2)}) copy-start(bf16[512]{0:T(512)(128)(2,1)} %copy-done.162) | copy-start | bytes 3076 | tf_op jit(solution)/shard_map/while
  1912.2 9.1 slice-start.3
  1912.3 9.1 slice-start.4
  1970.6 35.1 %collective-permute-start.4 = (bf16[64,512]{1,0:T(8,128)(2,1)}, bf16[64,512]{1,0:T(8,128)(2,1)S(1)}, u32[]{:S(2)}, u32[]{:S(2)}) collective-permute-start(bf16[64,512]{1,0:T(8,128)(2,1)} %get-tuple-element.7606), channel_id=1, source_target_pairs={{8,0},{16,8},{24,16},{9,1},{17,9},{25,17},{10,2},{18,10},{26,18},{... | collective-permute-start | bytes 196616 | tf_op jit(solution)/shard_map/while/body/eval_jaxpr/ppermute | solution.py:17
  2033.7 35.2 %collective-permute-start.5 = (bf16[64,512]{1,0:T(8,128)(2,1)}, bf16[64,512]{1,0:T(8,128)(2,1)S(1)}, u32[]{:S(2)}, u32[]{:S(2)}) collective-permute-start(bf16[64,512]{1,0:T(8,128)(2,1)} %get-tuple-element.7647), channel_id=1, source_target_pairs={{8,0},{16,8},{24,16},{9,1},{17,9},{25,17},{10,2},{18,10},{26,18},{... | collective-permute-start | bytes 196616 | tf_op jit(solution)/shard_map/while/body/eval_jaxpr/ppermute | solution.py:17
  2084.7 35.2 %collective-permute-start.5 = (bf16[64,512]{1,0:T(8,128)(2,1)}, bf16[64,512]{1,0:T(8,128)(2,1)S(1)}, u32[]{:S(2)}, u32[]{:S(2)}) collective-permute-start(bf16[64,512]{1,0:T(8,128)(2,1)} %get-tuple-element.7647), channel_id=1, source_target_pairs={{8,0},{16,8},{24,16},{9,1},{17,9},{25,17},{10,2},{18,10},{26,18},{... | collective-permute-start | bytes 196616 | tf_op jit(solution)/shard_map/while/body/eval_jaxpr/ppermute | solution.py:17
  2135.7 206.5 %collective-permute-start.5 = (bf16[64,512]{1,0:T(8,128)(2,1)}, bf16[64,512]{1,0:T(8,128)(2,1)S(1)}, u32[]{:S(2)}, u32[]{:S(2)}) collective-permute-start(bf16[64,512]{1,0:T(8,128)(2,1)} %get-tuple-element.7647), channel_id=1, source_target_pairs={{8,0},{16,8},{24,16},{9,1},{17,9},{25,17},{10,2},{18,10},{26,18},{... | collective-permute-start | bytes 196616 | tf_op jit(solution)/shard_map/while/body/eval_jaxpr/ppermute | solution.py:17
  2162.9 179.3 %copy-start.156 = (bf16[512]{0:T(512)(128)(2,1)S(1)}, bf16[512]{0:T(512)(128)(2,1)}, u32[]{:S(2)}) copy-start(bf16[512]{0:T(512)(128)(2,1)} %copy-done.155) | copy-start | bytes 3076 | tf_op jit(solution)/shard_map/while
  2162.9 179.3 %copy-start.165 = (bf16[512]{0:T(512)(128)(2,1)S(1)}, bf16[512]{0:T(512)(128)(2,1)}, u32[]{:S(2)}) copy-start(bf16[512]{0:T(512)(128)(2,1)} %copy-done.164) | copy-start | bytes 3076 | tf_op jit(solution)/shard_map/while
  2415.1 9.1 slice-start.6
  2415.1 9.1 slice-start.7
  2473.6 35.2 %collective-permute-start.5 = (bf16[64,512]{1,0:T(8,128)(2,1)}, bf16[64,512]{1,0:T(8,128)(2,1)S(1)}, u32[]{:S(2)}, u32[]{:S(2)}) collective-permute-start(bf16[64,512]{1,0:T(8,128)(2,1)} %get-tuple-element.7647), channel_id=1, source_target_pairs={{8,0},{16,8},{24,16},{9,1},{17,9},{25,17},{10,2},{18,10},{26,18},{... | collective-permute-start | bytes 196616 | tf_op jit(solution)/shard_map/while/body/eval_jaxpr/ppermute | solution.py:17
  2536.7 35.2 %collective-permute-start.6 = (bf16[64,512]{1,0:T(8,128)(2,1)}, bf16[64,512]{1,0:T(8,128)(2,1)S(1)}, u32[]{:S(2)}, u32[]{:S(2)}) collective-permute-start(bf16[64,512]{1,0:T(8,128)(2,1)} %get-tuple-element.7688), channel_id=1, source_target_pairs={{8,0},{16,8},{24,16},{9,1},{17,9},{25,17},{10,2},{18,10},{26,18},{... | collective-permute-start | bytes 196616 | tf_op jit(solution)/shard_map/while/body/eval_jaxpr/ppermute | solution.py:17
  2587.7 35.2 %collective-permute-start.6 = (bf16[64,512]{1,0:T(8,128)(2,1)}, bf16[64,512]{1,0:T(8,128)(2,1)S(1)}, u32[]{:S(2)}, u32[]{:S(2)}) collective-permute-start(bf16[64,512]{1,0:T(8,128)(2,1)} %get-tuple-element.7688), channel_id=1, source_target_pairs={{8,0},{16,8},{24,16},{9,1},{17,9},{25,17},{10,2},{18,10},{26,18},{... | collective-permute-start | bytes 196616 | tf_op jit(solution)/shard_map/while/body/eval_jaxpr/ppermute | solution.py:17
  2638.7 206.3 %collective-permute-start.6 = (bf16[64,512]{1,0:T(8,128)(2,1)}, bf16[64,512]{1,0:T(8,128)(2,1)S(1)}, u32[]{:S(2)}, u32[]{:S(2)}) collective-permute-start(bf16[64,512]{1,0:T(8,128)(2,1)} %get-tuple-element.7688), channel_id=1, source_target_pairs={{8,0},{16,8},{24,16},{9,1},{17,9},{25,17},{10,2},{18,10},{26,18},{... | collective-permute-start | bytes 196616 | tf_op jit(solution)/shard_map/while/body/eval_jaxpr/ppermute | solution.py:17
  2665.9 179.1 %copy-start.158 = (bf16[512]{0:T(512)(128)(2,1)S(1)}, bf16[512]{0:T(512)(128)(2,1)}, u32[]{:S(2)}) copy-start(bf16[512]{0:T(512)(128)(2,1)} %copy-done.157) | copy-start | bytes 3076 | tf_op jit(solution)/shard_map/while
  2665.9 179.1 %copy-start.167 = (bf16[512]{0:T(512)(128)(2,1)S(1)}, bf16[512]{0:T(512)(128)(2,1)}, u32[]{:S(2)}) copy-start(bf16[512]{0:T(512)(128)(2,1)} %copy-done.166) | copy-start | bytes 3076 | tf_op jit(solution)/shard_map/while
  2917.9 9.1 slice-start.9
  2917.9 9.1 slice-start.10
  2976.3 35.1 %collective-permute-start.6 = (bf16[64,512]{1,0:T(8,128)(2,1)}, bf16[64,512]{1,0:T(8,128)(2,1)S(1)}, u32[]{:S(2)}, u32[]{:S(2)}) collective-permute-start(bf16[64,512]{1,0:T(8,128)(2,1)} %get-tuple-element.7688), channel_id=1, source_target_pairs={{8,0},{16,8},{24,16},{9,1},{17,9},{25,17},{10,2},{18,10},{26,18},{... | collective-permute-start | bytes 196616 | tf_op jit(solution)/shard_map/while/body/eval_jaxpr/ppermute | solution.py:17
  3019.2 50.8 %copy-start.168 = (bf16[5,64,512]{2,1,0:T(8,128)(2,1)S(1)}, bf16[5,64,512]{2,1,0:T(8,128)(2,1)}, u32[]{:S(2)}) copy-start(bf16[5,64,512]{2,1,0:T(8,128)(2,1)} %get-tuple-element.5240) | copy-start | bytes 983044
  (403 other events, 1303.4 us)
Sparse Core Ops, SparseCore 0:
  3014.9 290.1 all-reduce.19
where the time goes:
time: 3350 us; the launch traced here: 3330 us
  waiting for transfers between devices  1060 us (32%)
  other arithmetic  672 us (20%)
  starting transfers between devices  527 us (16%)
  local copies, waits for them, and re-layouts  496 us (15%)
  matrix products  457 us (14%)
  loops' own time  52.5 us (2%)
  blocking collectives  44.3 us (1%)
    ppermute x32, waiting for transfers between devices, shifted(): return lax.ppermute(block, axis, route)  838 us
    ppermute x32, starting transfers between devices, shifted(): return lax.ppermute(block, axis, route)  527 us
    add x148, other arithmetic, backward_step(): grads = tuple((a + b for a, b in zip(grads, weight_grads)))  483 us
    dot_general x120, matrix products, product(): return jnp.dot(left, right, preferred_element_type=jnp.float32)  253 us
    psum x1, waiting for transfers between devices, body(): lax.psum((grad_attn_gain, grad_qkv_w, grad_attn_out, grad_ffn_gain, grad_...  227 us
    another operation x148, local copies, waits for them, and re-layouts  157 us
    sub x16, matrix products, attend(): jax.nn.softmax(jnp.where(allowed[None], scores, MASKED), axis=-1)  94 us
    dynamic_update_slice x48, local copies, waits for them, and re-layouts, put_row(): return lax.dynamic_update_index_in_dim(buffer, row, index, 0)  69.4 us
  transfers between devices with their start and end apart: 33, of which 6 were waited for; matrix products, arithmetic and copies ran while one was open for 17% of the time, Pallas kernels for 0%

commit v1 on v0

v1 whole, which is shorter than its diff:
```python
import jax
import jax.numpy as jnp
from jax import lax
from jax.experimental import pallas as pl
from jax.experimental.pallas import tpu as pltpu
from jax.sharding import PartitionSpec as P

HEADS = 8
HEAD_DIM = 64
EPS = 1e-06
MASKED = -1000000000.0
F32 = jnp.float32
BF16 = jnp.bfloat16
SQRT_2_PI = 0.7978845608028654
CUBIC = 0.044715
VMEM_LIMIT = 60 * 1024 * 1024


def nn(left, right):
    return lax.dot_general(left, right, (((1,), (0,)), ((), ())), preferred_element_type=F32)


def nt(left, right):
    return lax.dot_general(left, right, (((1,), (1,)), ((), ())), preferred_element_type=F32)


def wide(column_tile, width):
    copies = max(1, width // 128)
    if width < 128:
        return column_tile[:, :width]
    return jnp.concatenate([column_tile] * copies, axis=1)


def inverse_rms(values):
    return lax.rsqrt(jnp.mean(values * values, axis=0, keepdims=True) + EPS)


def lane_sums(values):
    total = values[:, :128]
    for at in range(128, values.shape[1], 128):
        total = total + values[:, at : at + 128]
    return total


def head_mask(rows, columns):
    row_head = lax.broadcasted_iota(jnp.int32, (rows, columns), 0) // HEAD_DIM
    column_head = lax.broadcasted_iota(jnp.int32, (rows, columns), 1) // HEAD_DIM
    return row_head == column_head


def norm_back(grad_normed, normed, scale, gain, gain_inverse):
    weighed = grad_normed * normed
    mean = jnp.mean(weighed, axis=0, keepdims=True)
    return scale * (grad_normed * gain - normed * gain_inverse * mean), weighed


def forward_kernel(
    flags,
    docs_ref,
    tok_ref,
    mem0_ref,
    init_ref,
    ga_ref,
    gf_ref,
    gw_ref,
    spread_ref,
    fold_ref,
    wqkv_ref,
    wao_ref,
    win_ref,
    wout_ref,
    ww_ref,
    wwo_ref,
    enc_ref,
    a1_ref,
    a1m_ref,
    q_ref,
    kt_ref,
    ktm_ref,
    v_ref,
    vm_ref,
    e_ref,
    em_ref,
    att_ref,
    a2_ref,
    z_ref,
    gp_ref,
    a3_ref,
    a3m_ref,
    qw_ref,
    kwt_ref,
    kwtm_ref,
    vw_ref,
    vwm_ref,
    ew_ref,
    ewm_ref,
    watt_ref,
    stat_ref,
    carry,
    bias,
    k_nat,
    km_nat,
    vt,
    vtm,
    hidden,
):
    step = pl.program_id(0)
    width = wao_ref.shape[0]
    seg = tok_ref.shape[1]
    slots = init_ref.shape[1]
    ff = win_ref.shape[0]

    @pl.when(step == 0)
    def _():
        carry[...] = mem0_ref[...].astype(F32)

    mem = jnp.where(flags[step] > 0, init_ref[...].astype(F32), carry[...])
    ga, gf, gw = ga_ref[...], gf_ref[...], gw_ref[...]

    docs = docs_ref[0].astype(F32)
    doc_rows = jnp.broadcast_to(docs, (128, seg)).T
    for at in range(0, seg, 128):
        bias[:, at : at + 128] = jnp.where(doc_rows == docs[:, at : at + 128], 0.0, MASKED)

    tokens = tok_ref[0].astype(F32).T
    r1 = inverse_rms(tokens)
    a1_ref[...] = (tokens * r1 * wide(ga, seg)).astype(BF16)
    rm = inverse_rms(mem)
    a1m_ref[0] = (mem * rm * ga[:, :slots]).astype(BF16)
    stat_ref[0, 0:1, :] = r1
    stat_ref[0, 4:5, :slots] = rm

    a1 = a1_ref[...]
    a1m = a1m_ref[0]
    q_ref[0] = (nn(wqkv_ref[:width, :], a1) * HEAD_DIM**-0.5).astype(BF16)
    kt = nn(wqkv_ref[width : 2 * width, :], a1).astype(BF16)
    kt_ref[0] = kt
    k_nat[...] = kt.T
    vt[...] = nn(wqkv_ref[2 * width :, :], a1).astype(BF16)
    v_ref[0] = vt[...].T
    ktm = nn(wqkv_ref[width : 2 * width, :], a1m).astype(BF16)
    ktm_ref[0] = ktm
    km_nat[...] = ktm.T
    vtm[...] = nn(wqkv_ref[2 * width :, :], a1m).astype(BF16)
    vm_ref[0] = vtm[...].T

    def pair(index, unused):
        lanes = pl.ds(pl.multiple_of(index * 128, 128), 128)
        keys = k_nat[:, lanes]
        mem_keys = km_nat[:, lanes]
        for half in range(2):
            head = index * 2 + half
            rows = pl.ds(pl.multiple_of(head * HEAD_DIM, HEAD_DIM), HEAD_DIM)
            queries = q_ref[0, rows, :]
            blank = jnp.zeros_like(queries)
            queries = jnp.concatenate([queries, blank] if half == 0 else [blank, queries], axis=0)
            for at in range(0, seg, 256):
                cols = slice(at, at + 256)
                scores = nn(keys, queries[:, cols]) + bias[:, cols]
                mem_scores = nn(mem_keys, queries[:, cols])
                top = jnp.maximum(
                    jnp.max(scores, axis=0, keepdims=True),
                    jnp.max(mem_scores, axis=0, keepdims=True),
                )
                raised = jnp.exp(scores - top)
                mem_raised = jnp.exp(mem_scores - top)
                inverse = 1.0 / (
                    jnp.sum(raised, axis=0, keepdims=True)
                    + jnp.sum(mem_raised, axis=0, keepdims=True)
                )
                raised = raised.astype(BF16)
                mem_raised = mem_raised.astype(BF16)
                e_ref[0, head, :, cols] = raised
                em_ref[0, rows, cols] = mem_raised
                mixed = nn(vt[rows, :], raised) + nn(vtm[rows, :], mem_raised)
                att_ref[rows, cols] = (mixed * inverse).astype(BF16)
                stat_ref[0, pl.ds(8 + head, 1), cols] = inverse
        return unused

    lax.fori_loop(0, HEADS // 2, pair, 0)

    h1 = tok_ref[0].astype(F32).T + nn(wao_ref[...], att_ref[...])
    r2 = inverse_rms(h1)
    stat_ref[0, 1:2, :] = r2
    a2_ref[...] = (h1 * r2 * wide(gf, seg)).astype(BF16)
    hidden[...] = h1
    a2 = a2_ref[...]
    for at in range(0, ff, 512):
        upper = nn(win_ref[at : at + 512, :], a2)
        square = upper * upper
        bent = jnp.tanh(upper * (SQRT_2_PI + (SQRT_2_PI * CUBIC) * square))
        cdf = 0.5 + 0.5 * bent
        z_ref[at : at + 512, :] = (upper * cdf).astype(BF16)
        slope = (0.5 * SQRT_2_PI) + (1.5 * SQRT_2_PI * CUBIC) * square
        gp_ref[0, at : at + 512, :] = (cdf + upper * (1.0 - bent * bent) * slope).astype(BF16)
    enc = hidden[...] + nn(wout_ref[...], z_ref[...])
    enc_ref[0, :seg, :] = enc.T.astype(BF16)
    r3 = inverse_rms(enc)
    stat_ref[0, 2:3, :] = r3
    a3_ref[...] = (enc * r3 * wide(gw, seg)).astype(BF16)
    a3m_ref[0] = (mem * rm * gw[:, :slots]).astype(BF16)
    a3 = a3_ref[...]
    a3m = a3m_ref[0]

    kwt = nn(ww_ref[width : 2 * width, :], a3).astype(BF16)
    kwt_ref[0] = kwt
    kw = kwt.T
    vwt = nn(ww_ref[2 * width :, :], a3).astype(BF16)
    vw_ref[0] = vwt.T
    kwtm = nn(ww_ref[width : 2 * width, :], a3m).astype(BF16)
    kwtm_ref[0] = kwtm
    vwtm = nn(ww_ref[2 * width :, :], a3m).astype(BF16)
    vwm_ref[0] = vwtm.T
    qwt = (nn(ww_ref[:width, :], a3m) * HEAD_DIM**-0.5).astype(BF16)
    own = head_mask(width, HEADS * slots)
    qw = jnp.where(own, nn(qwt, spread_ref[...]), 0.0).astype(BF16)
    qw_ref[0] = qw
    scores = nn(kw, qw)
    mem_scores = nn(kwtm.T, qw)
    slot_row = lax.broadcasted_iota(jnp.int32, mem_scores.shape, 0)
    slot_col = lax.broadcasted_iota(jnp.int32, mem_scores.shape, 1) % slots
    mem_scores = jnp.where(slot_row == slot_col, mem_scores, MASKED)
    top = jnp.maximum(
        jnp.max(scores, axis=0, keepdims=True), jnp.max(mem_scores, axis=0, keepdims=True)
    )
    raised = jnp.exp(scores - top)
    mem_raised = jnp.exp(mem_scores - top)
    inverse = 1.0 / (
        jnp.sum(raised, axis=0, keepdims=True) + jnp.sum(mem_raised, axis=0, keepdims=True)
    )
    stat_ref[0, 3:4, :] = inverse
    raised = raised.astype(BF16)
    mem_raised = mem_raised.astype(BF16)
    ew_ref[0] = raised
    ewm_ref[0] = mem_raised
    mixed = (nn(vwt, raised) + nn(vwtm, mem_raised)) * inverse
    watt = nn(jnp.where(own, mixed, 0.0).astype(BF16), fold_ref[...]).astype(BF16)
    watt_ref[0] = watt
    new_mem = (mem + nn(wwo_ref[...], watt)).astype(BF16).astype(F32)
    carry[...] = new_mem
    enc_ref[0, seg:, :] = new_mem.T.astype(BF16)


def chain_kernel(
    flags,
    gout_ref,
    carry0_ref,
    ga_ref,
    gf_ref,
    gw_ref,
    gai_ref,
    gfi_ref,
    gwi_ref,
    spread_ref,
    fold_ref,
    wqkv_ref,
    wao_ref,
    win_ref,
    wout_ref,
    ww_ref,
    wwo_ref,
    a1m_ref,
    q_ref,
    vm_ref,
    em_ref,
    att_ref,
    a2_ref,
    gp_ref,
    a3_ref,
    a3m_ref,
    qw_ref,
    kwt_ref,
    kwtm_ref,
    vw_ref,
    vwm_ref,
    ew_ref,
    ewm_ref,
    stat_ref,
    bm_ref,
    gwkv_ref,
    gwm_ref,
    bf_ref,
    gu_ref,
    ba_ref,
    gh_ref,
    do_ref,
    dd_ref,
    dsm_ref,
    gkvm_ref,
    init_ref,
    gains_ref,
    sent_ref,
    carry,
):
    step = pl.program_id(0)
    steps = pl.num_programs(0)
    place = steps - 1 - step
    width = wao_ref.shape[0]
    ff = wout_ref.shape[0]
    seg = q_ref.shape[2]
    slots = a1m_ref.shape[2]
    reset = flags[place] > 0

    @pl.when(step == 0)
    def _():
        carry[...] = carry0_ref[...].astype(F32)
        init_ref[...] = jnp.zeros_like(init_ref)
        gains_ref[...] = jnp.zeros_like(gains_ref)

    ga, gf, gw = ga_ref[...], gf_ref[...], gw_ref[...]
    gai, gfi, gwi = gai_ref[...], gfi_ref[...], gwi_ref[...]
    own = head_mask(width, HEADS * slots)
    rm = stat_ref[0, 4:5, :slots]

    grad_mem = gout_ref[0, seg:, :].astype(F32).T + carry[...]
    branch_mem = grad_mem.astype(BF16)
    bm_ref[0] = branch_mem
    grad_watt = nn(wwo_ref[...], branch_mem).astype(BF16)
    inverse = stat_ref[0, 3:4, :]
    scaled = (jnp.where(own, nn(grad_watt, spread_ref[...]), 0.0) * inverse).astype(BF16)
    raised = ew_ref[0].astype(F32)
    mem_raised = ewm_ref[0].astype(F32)
    grad_probs = nn(vw_ref[0], scaled)
    mem_grad_probs = nn(vwm_ref[0], scaled)
    dots = (
        jnp.sum(raised * grad_probs, axis=0, keepdims=True)
        + jnp.sum(mem_raised * mem_grad_probs, axis=0, keepdims=True)
    ) * inverse
    grad_scores = (raised * (grad_probs - dots)).astype(BF16)
    mem_grad_scores = (mem_raised * (mem_grad_probs - dots)).astype(BF16)
    gwkv_ref[:width, :] = nt(qw_ref[0], grad_scores).astype(BF16)
    gwkv_ref[width:, :] = nt(scaled, ew_ref[0]).astype(BF16)
    grad_q = (nn(kwt_ref[0], grad_scores) + nn(kwtm_ref[0], mem_grad_scores)) * HEAD_DIM**-0.5
    gwm_ref[0, :width, :] = nn(jnp.where(own, grad_q, 0.0).astype(BF16), fold_ref[...]).astype(BF16)
    gwm_ref[0, width : 2 * width, :] = nt(qw_ref[0], mem_grad_scores).astype(BF16)
    gwm_ref[0, 2 * width :, :] = nt(scaled, ewm_ref[0]).astype(BF16)

    grad_a3 = nn(ww_ref[:, width:], gwkv_ref[...])
    grad_a3m = nn(ww_ref[...], gwm_ref[0])
    part, weighed = norm_back(
        grad_a3, a3_ref[...].astype(F32), stat_ref[0, 2:3, :], wide(gw, seg), wide(gwi, seg)
    )
    mem_part, mem_weighed = norm_back(
        grad_a3m, a3m_ref[0].astype(F32), rm, gw[:, :slots], gwi[:, :slots]
    )
    gains_ref[2] += lane_sums(weighed)
    gains_ref[2, :, :slots] += mem_weighed
    grad_mem_in = grad_mem + mem_part
    gh_ref[0] = gout_ref[0, :seg, :].astype(F32).T + part

    bf_ref[...] = gh_ref[0].astype(BF16)
    branch = bf_ref[...]
    for at in range(0, ff, 512):
        grad_z = nn(wout_ref[at : at + 512, :], branch)
        gu_ref[at : at + 512, :] = (grad_z * gp_ref[0, at : at + 512, :].astype(F32)).astype(BF16)
    grad_a2 = nn(win_ref[...], gu_ref[...])
    part, weighed = norm_back(
        grad_a2, a2_ref[...].astype(F32), stat_ref[0, 1:2, :], wide(gf, seg), wide(gfi, seg)
    )
    gains_ref[1] += lane_sums(weighed)
    gh_ref[0] += part

    ba_ref[...] = gh_ref[0].astype(BF16)
    grad_att = nn(wao_ref[...], ba_ref[...]).astype(BF16)
    products = grad_att.astype(F32) * att_ref[...].astype(F32)
    rows = []
    dots = []
    for head in range(HEADS):
        span = slice(head * HEAD_DIM, (head + 1) * HEAD_DIM)
        inverse = stat_ref[0, 8 + head : 9 + head, :]
        dots.append(jnp.sum(products[span, :], axis=0, keepdims=True) * inverse)
        rows.append((grad_att[span, :].astype(F32) * inverse).astype(BF16))
    scaled = jnp.concatenate(rows, axis=0)
    do_ref[0] = scaled
    dd_ref[0] = jnp.concatenate(dots, axis=0)
    mem_values = jnp.concatenate([vm_ref[0].astype(F32)] * HEADS, axis=0)
    mem_values = jnp.where(own, mem_values, 0.0).astype(BF16)
    grad_probs = nn(mem_values, scaled)
    parts = []
    for head in range(HEADS):
        span = slice(head * slots, (head + 1) * slots)
        parts.append(
            (em_ref[0, span, :].astype(F32) * (grad_probs[span, :] - dots[head])).astype(BF16)
        )
    grad_scores = jnp.concatenate(parts, axis=0)
    dsm_ref[0] = grad_scores
    grad_k = jnp.where(own, nt(q_ref[0], grad_scores), 0.0).astype(BF16)
    grad_v = jnp.where(own, nt(scaled, em_ref[0]), 0.0).astype(BF16)
    gkvm_ref[0, :width, :] = nn(grad_k, fold_ref[...]).astype(BF16)
    gkvm_ref[0, width:, :] = nn(grad_v, fold_ref[...]).astype(BF16)
    grad_a1m = nn(wqkv_ref[:, width:], gkvm_ref[0])
    mem_part, mem_weighed = norm_back(
        grad_a1m, a1m_ref[0].astype(F32), rm, ga[:, :slots], gai[:, :slots]
    )
    gains_ref[0, :, :slots] += mem_weighed
    grad_mem_in = grad_mem_in + mem_part
    init_ref[...] += jnp.where(reset, grad_mem_in, 0.0)
    carry[...] = jnp.where(reset, 0.0, grad_mem_in).astype(BF16).astype(F32)
    sent_ref[...] = carry[...].astype(BF16)


def attention_kernel(
    do_ref,
    dd_ref,
    dsm_ref,
    gh_ref,
    q_ref,
    kt_ref,
    ktm_ref,
    v_ref,
    e_ref,
    a1_ref,
    stat_ref,
    ga_ref,
    gai_ref,
    wqkv_ref,
    gqkv_ref,
    gtok_ref,
    gain_ref,
    grad_scores,
):
    step = pl.program_id(0)
    width = wqkv_ref.shape[0]
    seg = q_ref.shape[2]

    @pl.when(step == 0)
    def _():
        gain_ref[...] = jnp.zeros_like(gain_ref)

    def pair(index, unused):
        lanes = pl.ds(pl.multiple_of(index * 128, 128), 128)
        values = v_ref[0, :, lanes]
        for half in range(2):
            head = index * 2 + half
            base = pl.multiple_of(head * HEAD_DIM, HEAD_DIM)
            rows = pl.ds(base, HEAD_DIM)
            key_rows = pl.ds(width + base, HEAD_DIM)
            value_rows = pl.ds(2 * width + base, HEAD_DIM)
            grads = do_ref[0, rows, :]
            blank = jnp.zeros_like(grads)
            padded = jnp.concatenate([grads, blank] if half == 0 else [blank, grads], axis=0)
            dots = dd_ref[0, pl.ds(head, 1), :]
            for at in range(0, seg, 256):
                cols = slice(at, at + 256)
                grad_probs = nn(values, padded[:, cols])
                raised = e_ref[0, head, :, cols].astype(F32)
                inner = (raised * (grad_probs - dots[:, cols])).astype(BF16)
                grad_scores[half, :, cols] = inner
                grad_q = nn(kt_ref[0, rows, :], inner) + nn(ktm_ref[0, rows, :], dsm_ref[0, rows, cols])
                gqkv_ref[rows, cols] = (grad_q * HEAD_DIM**-0.5).astype(BF16)
            gqkv_ref[key_rows, :] = nt(q_ref[0, rows, :], grad_scores[half]).astype(BF16)
            gqkv_ref[value_rows, :] = nt(grads, e_ref[0, head]).astype(BF16)
        return unused

    lax.fori_loop(0, HEADS // 2, pair, 0)
    grad_a1 = nn(wqkv_ref[...], gqkv_ref[...])
    part, weighed = norm_back(
        grad_a1,
        a1_ref[...].astype(F32),
        stat_ref[0, 0:1, :],
        wide(ga_ref[...], seg),
        wide(gai_ref[...], seg),
    )
    gain_ref[...] += lane_sums(weighed)
    gtok_ref[0] = (gh_ref[0] + part).T.astype(BF16)


def whole(array):
    zeros = (0,) * array.ndim
    return pl.BlockSpec(array.shape, lambda *unused: zeros, pipeline_mode=pl.Buffered(1))


def params():
    return pltpu.CompilerParams(
        dimension_semantics=("arbitrary",), vmem_limit_bytes=VMEM_LIMIT
    )


def forward_chain(rows, docs, flags, mem0, consts, w):
    segs, seg, width = rows.shape[0], rows.shape[1], rows.shape[2]
    slots = mem0.shape[1]
    ff = w["in_t"].shape[0]
    flat = lambda height: (jax.ShapeDtypeStruct((height, segs * seg), BF16), pl.BlockSpec((height, seg), lambda s, f: (0, s)))

    def stack(*shape, dtype=BF16):
        tail = (0,) * len(shape)
        return (
            jax.ShapeDtypeStruct((segs,) + shape, dtype),
            pl.BlockSpec((1,) + shape, lambda s, f: (s,) + tail),
        )

    outs = dict(
        enc=stack(seg + slots, width),
        a1=flat(width),
        a1m=stack(width, slots),
        q=stack(width, seg),
        kt=stack(width, seg),
        ktm=stack(width, slots),
        v=stack(seg, width),
        vm=stack(slots, width),
        e=stack(HEADS, seg, seg),
        em=stack(HEADS * slots, seg),
        att=flat(width),
        a2=flat(width),
        z=flat(ff),
        gp=stack(ff, seg),
        a3=flat(width),
        a3m=stack(width, slots),
        qw=stack(width, HEADS * slots),
        kwt=stack(width, seg),
        kwtm=stack(width, slots),
        vw=stack(seg, width),
        vwm=stack(slots, width),
        ew=stack(seg, HEADS * slots),
        ewm=stack(slots, HEADS * slots),
        watt=stack(width, slots),
        stat=stack(16, seg, dtype=F32),
    )
    fixed = [
        mem0,
        consts["init_t"],
        consts["ga"],
        consts["gf"],
        consts["gw"],
        consts["spread"],
        consts["fold"],
        w["qkv_t"],
        w["ao_t"],
        w["in_t"],
        w["out_t"],
        w["write_t"],
        w["wo_t"],
    ]
    results = pl.pallas_call(
        forward_kernel,
        grid_spec=pltpu.PrefetchScalarGridSpec(
            num_scalar_prefetch=1,
            grid=(segs,),
            in_specs=[
                pl.BlockSpec((1, 1, seg), lambda s, f: (s, 0, 0)),
                pl.BlockSpec((1, seg, width), lambda s, f: (s, 0, 0)),
            ]
            + [whole(a) for a in fixed],
            out_specs=[spec for _, spec in outs.values()],
            scratch_shapes=[
                pltpu.VMEM((width, slots), F32),
                pltpu.VMEM((seg, seg), F32),
                pltpu.VMEM((seg, width), BF16),
                pltpu.VMEM((slots, width), BF16),
                pltpu.VMEM((width, seg), BF16),
                pltpu.VMEM((width, slots), BF16),
                pltpu.VMEM((width, seg), F32),
            ],
        ),
        out_shape=[shape for shape, _ in outs.values()],
        compiler_params=params(),
        name="forward_chain",
    )(flags, docs, rows, *fixed)
    return dict(zip(outs, results))


def backward_chain(kept, gout, flags, carry0, consts, w):
    segs = gout.shape[0]
    width, slots = kept["a1m"].shape[1:]
    seg = kept["q"].shape[2]
    ff = kept["gp"].shape[1]
    last = segs - 1

    def flat(height):
        return (
            jax.ShapeDtypeStruct((height, segs * seg), BF16),
            pl.BlockSpec((height, seg), lambda s, f: (0, last - s)),
        )

    def stack(*shape, dtype=BF16):
        tail = (0,) * len(shape)
        return (
            jax.ShapeDtypeStruct((segs,) + shape, dtype),
            pl.BlockSpec((1,) + shape, lambda s, f: (last - s,) + tail),
        )

    def single(*shape, dtype=F32):
        tail = (0,) * len(shape)
        return (jax.ShapeDtypeStruct(shape, dtype), pl.BlockSpec(shape, lambda s, f: tail))

    outs = dict(
        bm=stack(width, slots),
        gwkv=flat(2 * width),
        gwm=stack(3 * width, slots),
        bf=flat(width),
        gu=flat(ff),
        ba=flat(width),
        gh=stack(width, seg, dtype=F32),
        do=stack(width, seg),
        dd=stack(HEADS, seg, dtype=F32),
        dsm=stack(HEADS * slots, seg),
        gkvm=stack(2 * width, slots),
        init=single(width, slots),
        gains=single(3, width, 128),
        sent=single(width, slots, dtype=BF16),
    )
    fixed = [
        carry0,
        consts["ga"],
        consts["gf"],
        consts["gw"],
        consts["gai"],
        consts["gfi"],
        consts["gwi"],
        consts["spread"],
        consts["fold"],
        w["qkv"],
        w["ao"],
        w["in"],
        w["out"],
        w["write"],
        w["wo"],
    ]
    blocked = ["a1m", "q", "vm", "em", "att", "a2", "gp", "a3", "a3m", "qw", "kwt", "kwtm", "vw", "vwm", "ew", "ewm", "stat"]

    def spec_of(array):
        if array.ndim == 2:
            return pl.BlockSpec((array.shape[0], seg), lambda s, f: (0, last - s))
        tail = (0,) * (array.ndim - 1)
        return pl.BlockSpec((1,) + array.shape[1:], lambda s, f: (last - s,) + tail)

    results = pl.pallas_call(
        chain_kernel,
        grid_spec=pltpu.PrefetchScalarGridSpec(
            num_scalar_prefetch=1,
            grid=(segs,),
            in_specs=[spec_of(gout)]
            + [whole(a) for a in fixed]
            + [spec_of(kept[name]) for name in blocked],
            out_specs=[spec for _, spec in outs.values()],
            scratch_shapes=[pltpu.VMEM((width, slots), F32)],
        ),
        out_shape=[shape for shape, _ in outs.values()],
        compiler_params=params(),
        name="backward_chain",
    )(flags, gout, *fixed, *[kept[name] for name in blocked])
    return dict(zip(outs, results))


def attention_back(kept, grads, consts, w):
    segs, width, seg = kept["q"].shape

    def spec_of(array):
        if array.ndim == 2:
            return pl.BlockSpec((array.shape[0], seg), lambda s: (0, s))
        tail = (0,) * (array.ndim - 1)
        return pl.BlockSpec((1,) + array.shape[1:], lambda s: (s,) + tail)

    blocked = [grads["do"], grads["dd"], grads["dsm"], grads["gh"]] + [
        kept[name] for name in ("q", "kt", "ktm", "v", "e", "a1", "stat")
    ]
    fixed = [consts["ga"], consts["gai"], w["qkv"]]
    return pl.pallas_call(
        attention_kernel,
        grid=(segs,),
        in_specs=[spec_of(a) for a in blocked] + [whole(a) for a in fixed],
        out_specs=[
            pl.BlockSpec((3 * width, seg), lambda s: (0, s)),
            pl.BlockSpec((1, seg, width), lambda s: (s, 0, 0)),
            pl.BlockSpec((width, 128), lambda s: (0, 0)),
        ],
        out_shape=[
            jax.ShapeDtypeStruct((3 * width, segs * seg), BF16),
            jax.ShapeDtypeStruct((segs, seg, width), BF16),
            jax.ShapeDtypeStruct((width, 128), F32),
        ],
        scratch_shapes=[pltpu.VMEM((2, seg, seg), BF16)],
        compiler_params=params(),
        name="attention_back",
    )(*blocked, *fixed)


def swap_pairs(value, axis, mask):
    size = lax.axis_size(axis)
    return lax.ppermute(value, axis, [(i, i ^ mask) for i in range(size)])


def bits_of(axis):
    size = lax.axis_size(axis)
    return [(axis, 1 << at) for at in range(size.bit_length() - 1)]


def summed(value, order):
    for axis, mask in order:
        half = value.shape[0] // 2
        high = (lax.axis_index(axis) // mask) % 2
        sent = lax.dynamic_slice_in_dim(value, (1 - high) * half, half, 0)
        held = lax.dynamic_slice_in_dim(value, high * half, half, 0)
        value = held + swap_pairs(sent, axis, mask)
    for axis, mask in reversed(order):
        high = (lax.axis_index(axis) // mask) % 2
        other = swap_pairs(value, axis, mask)
        low_part = jnp.where(high == 0, value, other)
        high_part = jnp.where(high == 0, other, value)
        value = jnp.concatenate([low_part, high_part], axis=0)
    return value


def to_streams(value, chunks):
    place = lax.axis_index("section")
    if chunks == 1:
        sections = lax.axis_size("section")
        parts = [lax.dynamic_index_in_dim(value, place, 0, keepdims=False)]
        for mask in range(1, sections):
            sent = lax.dynamic_index_in_dim(value, place ^ mask, 0, keepdims=False)
            parts.append(swap_pairs(sent, "section", mask))
        stacked = jnp.stack(parts)
        return jnp.stack(
            [lax.dynamic_index_in_dim(stacked, place ^ at, 0, keepdims=False) for at in range(sections)]
        )
    gathered = lax.all_gather(value, "section")
    own = lax.dynamic_index_in_dim(gathered, place // chunks, 1, keepdims=False)
    count = gathered.shape[0] // chunks
    return lax.dynamic_slice_in_dim(own, (place % chunks) * count, count, 0)


def to_segments(value, chunks):
    if chunks == 1:
        return to_streams(value, 1)
    place = lax.axis_index("section")
    gathered = lax.all_gather(value, "section")
    sections = gathered.shape[0]
    count = value.shape[0]
    by_stream = gathered.reshape((sections // chunks, chunks * count) + value.shape[1:])
    return lax.dynamic_index_in_dim(by_stream, place, 1, keepdims=False)


def body(
    tokens,
    doc_ids,
    reset_flags,
    attn_gain,
    w_qkv,
    w_attn_out,
    ffn_gain,
    w_in,
    w_out,
    write_gain,
    w_write,
    w_write_out,
    init_memory,
    out_grad,
    memory_grad,
):
    streams, _, seg, width = tokens.shape
    slots = init_memory.shape[0]
    ff = w_in.shape[1]
    sections = lax.axis_size("section")
    chunks = sections // streams
    place = lax.axis_index("section")

    def lanes_of(gain):
        return jnp.broadcast_to(gain.astype(F32)[:, None], (width, 128))

    spread = (jnp.arange(slots)[:, None] == jnp.arange(HEADS * slots)[None, :] % slots).astype(BF16)
    consts = dict(
        init_t=init_memory.T,
        ga=lanes_of(attn_gain),
        gf=lanes_of(ffn_gain),
        gw=lanes_of(write_gain),
        spread=spread,
        fold=spread.T,
    )
    for name in ("ga", "gf", "gw"):
        consts[name + "i"] = 1.0 / consts[name]
    w = dict(
        qkv=w_qkv,
        ao=w_attn_out,
        out=w_out,
        write=w_write,
        wo=w_write_out,
        qkv_t=w_qkv.T,
        ao_t=w_attn_out.T,
        in_t=w_in.T,
        out_t=w_out.T,
        write_t=w_write.T,
        wo_t=w_write_out.T,
    )
    w["in"] = w_in

    marks = jnp.concatenate(
        [doc_ids[:, 0], jnp.broadcast_to(reset_flags, (streams, seg))], axis=1
    ).reshape(streams, 2, seg)
    marks = jnp.pad(marks, ((0, 0), (0, 14), (0, 0))).astype(BF16)
    own = to_streams(jnp.concatenate([tokens[:, 0], marks], axis=1), chunks)
    rows = own[:, :seg]
    docs = own[:, seg : seg + 1]
    flags = own[:, seg + 1, 0].astype(jnp.int32)
    gout = to_streams(jnp.concatenate([out_grad[:, 0], memory_grad[:, 0]], axis=1), chunks)

    arriving = jnp.zeros((width, slots), BF16)
    for turn in range(chunks):
        kept = forward_chain(rows, docs, flags, arriving, consts, w)
        if turn < chunks - 1:
            last = kept["enc"][-1, seg:, :].T
            arriving = lax.ppermute(last, "section", [(i, i + 1) for i in range(sections - 1)])

    returned = to_segments(kept["enc"], chunks)

    returning = jnp.zeros((width, slots), BF16)
    for turn in range(chunks):
        grads = backward_chain(kept, gout, flags, returning, consts, w)
        if turn < chunks - 1:
            returning = lax.ppermute(grads["sent"], "section", [(i + 1, i) for i in range(sections - 1)])

    gqkv, gtok, gain_attn = attention_back(kept, grads, consts, w)
    token_grads = to_segments(gtok, chunks)

    def weight(left, right):
        return lax.dot_general(left, right, (((1,), (1,)), ((), ())), preferred_element_type=F32)

    def weight_mem(left, right):
        return jnp.einsum("sft,sgt->fg", left, right, preferred_element_type=F32)

    grad_out = weight(kept["z"], grads["bf"]).astype(BF16)
    grad_in = weight(kept["a2"], grads["gu"]).astype(BF16)
    grad_write = weight_mem(kept["a3m"], grads["gwm"])
    grad_write = jnp.concatenate(
        [grad_write[:, :width], grad_write[:, width:] + weight(kept["a3"], grads["gwkv"])], axis=1
    )
    grad_wo = weight_mem(kept["watt"], grads["bm"])
    grad_ao = weight(kept["att"], grads["ba"])
    grad_qkv = weight(kept["a1"], gqkv)
    grad_qkv = jnp.concatenate(
        [grad_qkv[:, :width], grad_qkv[:, width:] + weight_mem(kept["a1m"], grads["gkvm"])], axis=1
    )
    gains = jnp.sum(grads["gains"], axis=2)
    gains = gains + jnp.stack([jnp.sum(gain_attn, axis=1), jnp.zeros(width), jnp.zeros(width)])
    gains = gains / jnp.stack([attn_gain, ffn_gain, write_gain]).astype(F32)
    extras = jnp.concatenate([grads["init"].T.reshape(-1), gains.reshape(-1)])
    pad = (-extras.shape[0]) % (width * 128)
    extras = jnp.pad(extras, (0, pad)).reshape(width, -1)

    section_bits = bits_of("section")
    dp_bits = bits_of("dp")
    order = section_bits[:1] + dp_bits[:1] + section_bits[1:] + dp_bits[1:]
    other = section_bits + dp_bits
    group_out = summed(grad_out, order)
    group_in = summed(grad_in, other)
    group_write = summed(jnp.concatenate([grad_write, grad_wo], axis=1).astype(BF16), order)
    group_qkv = summed(jnp.concatenate([grad_qkv, grad_ao, extras], axis=1).astype(BF16), other)

    extras = group_qkv[:, 4 * width :].astype(F32).reshape(-1)
    cut = slots * width
    init_grad = extras[:cut].reshape(slots, width)
    gains = extras[cut : cut + 3 * width].reshape(3, width)
    return (
        returned[:, None, :seg],
        returned[:, None, seg:],
        token_grads[:, None].astype(F32),
        gains[0],
        group_qkv[:, : 3 * width].astype(F32),
        group_qkv[:, 3 * width : 4 * width].astype(F32),
        gains[1],
        group_in.astype(F32),
        group_out.astype(F32),
        gains[2],
        group_write[:, : 3 * width].astype(F32),
        group_write[:, 3 * width :].astype(F32),
        init_grad,
    )


def solution(mesh):
    local = P("dp", "section")
    return jax.shard_map(
        body,
        mesh=mesh,
        in_specs=(local,) * 3 + (P(),) * 10 + (local,) * 2,
        out_specs=(local,) * 3 + (P(),) * 10,
        check_vma=False,
    )
```

time: 3350 us -> 417 us (0.12)
  waiting for transfers between devices: 1060 us -> 86.5 us
  other arithmetic: 672 us -> 41.5 us
  starting transfers between devices: 527 us -> 60.4 us
  local copies, waits for them, and re-layouts: 496 us -> 29.7 us
  matrix products: 457 us -> 27.7 us
  Pallas kernels: 0 us -> 165 us
  loops' own time: 52.5 us -> 0 us
  blocking collectives: 44.3 us -> 0 us
    ppermute x32 -> x52, waiting for transfers between devices: 838 us -> 86.5 us  [swap_pairs(): return lax.ppermute(value, axis, [(i, i ^ mask) for i in range(size)])]
    add x164 -> x20, other arithmetic: 492 us -> 2.45 us  [summed(): value = held + swap_pairs(sent, axis, mask)]
    ppermute x32 -> x52, starting transfers between devices: 527 us -> 60.4 us  [swap_pairs(): return lax.ppermute(value, axis, [(i, i ^ mask) for i in range(size)])]
    dot_general x168 -> x8, matrix products: 363 us -> 27.7 us  [the longest x5 23.9 us: weight(): lax.dot_general(left, right, (((1,), (1,)), ((), ())), preferred_element_...]
    psum x1 -> x0, waiting for transfers between devices: 227 us -> none  [body(): lax.psum((grad_attn_gain, grad_qkv_w, grad_attn_out, grad_ffn_gain, grad_...]
    pallas_call x0 -> x3, Pallas kernels: none -> 165 us  [the longest x1 79.7 us: forward_chain(): pl.pallas_call(forward_kernel, grid_spec=pltpu.PrefetchScalarGridSpec(num...]
    another operation x148 -> x5, local copies, waits for them, and re-layouts: 157 us -> 0.88 us
    sub x16 -> x0, matrix products: 94 us -> none  [attend(): jax.nn.softmax(jnp.where(allowed[None], scores, MASKED), axis=-1)]
  transfers between devices with their start and end apart: 33 -> 52, of which waited for: 6 -> 19; matrix products, arithmetic and copies ran while one was open for 17% -> 21% of each run, Pallas kernels for 0% -> 40%
where the time goes in v1:
time: 417 us; the launch traced here: 413 us
  Pallas kernels  165 us (40%)
  waiting for transfers between devices  86.5 us (21%)
  starting transfers between devices  60.4 us (14%)
  other arithmetic  41.5 us (10%)
  local copies, waits for them, and re-layouts  29.7 us (7%)
  matrix products  27.7 us (7%)
    ppermute x52, waiting for transfers between devices, swap_pairs(): return lax.ppermute(value, axis, [(i, i ^ mask) for i in range(size)])  86.5 us
    pallas_call x1, Pallas kernels, forward_chain(): pl.pallas_call(forward_kernel, grid_spec=pltpu.PrefetchScalarGridSpec(num...  79.7 us
    ppermute x52, starting transfers between devices, swap_pairs(): return lax.ppermute(value, axis, [(i, i ^ mask) for i in range(size)])  60.4 us
    pallas_call x1, Pallas kernels, backward_chain(): pl.pallas_call(chain_kernel, grid_spec=pltpu.PrefetchScalarGridSpec(num_s...  46.5 us
    pallas_call x1, Pallas kernels, attention_back(): pl.pallas_call(attention_kernel, grid=(segs,), in_specs=[spec_of(a) for a...  38.4 us
    dot_general x5, matrix products, weight(): lax.dot_general(left, right, (((1,), (1,)), ((), ())), preferred_element_...  23.9 us
    unnamed x71, local copies, waits for them, and re-layouts  18.4 us
  transfers between devices with their start and end apart: 52, of which 19 were waited for; matrix products, arithmetic and copies ran while one was open for 21% of the time, Pallas kernels for 40%

profile of v1, /device:TPU:0, one launch (start us, length us, event | category | flops | bytes accessed | tf_op | source)
XLA Modules:
  0.0 412.9 jit_solution(9132006527273699072)
XLA Ops:
  2.2 3.1 fusion.16
  5.7 2.5 collective-permute-start.1
  10.0 1.9 collective-permute-start.7
  12.1 2.5 copy.48
  14.6 4.0 copy.49
  18.7 1.6 copy.50
  20.3 1.6 copy.46
  26.4 6.5 %collective-permute-done.2 = bf16[528,512]{1,0:T(8,128)(2,1)} collective-permute-done((bf16[528,512]{1,0:T(8,128)(2,1)}, bf16[528,512]{1,0:T(8,128)(2,1)}, u32[]{:S(2)}, u32[]{:S(2)}) %collective-permute-start.2) | collective-permute-done | bytes 540704 | tf_op jit(solution)/shard_map/ppermute | solution.py:680
  32.9 1.6 pad_maximum_fusion.5
  36.0 1.5 pad_maximum_fusion.6.tok_ref
  40.7 79.7 %forward_chain.1 = (bf16[4,576,512]{2,1,0:T(8,128)(2,1)}, bf16[512,2048]{1,0:T(8,128)(2,1)}, bf16[4,512,64]{2,1,0:T(8,128)(2,1)}, bf16[4,512,512]{2,1,0:T(8,128)...) custom-call(s32[4]{0:T(128)} %fusion.34.flags, ...), custom_call_target="tpu_custom_call" | custom-call | tf_op jit(solution)/shard_map/forward_chain/pallas_call | solution.py:534
  120.3 3.0 constant_dynamic-slice_fusion.29
  123.5 1.9 collective-permute-start.4
  125.4 1.5 pad_maximum_fusion.2
  127.1 1.7 pad_maximum_fusion.3.gout_ref
  131.4 46.5 %backward_chain.1 = (bf16[4,512,64]{2,1,0:T(8,128)(2,1)}, bf16[1024,2048]{1,0:T(8,128)(2,1)}, bf16[4,1536,64]{2,1,0:T(8,128)(2,1)}, bf16[512,2048]{1,0:T(8,128)(...) custom-call(s32[4]{0:T(128)} %fusion.34.flags, ...), custom_call_target="tpu_custom_call" | custom-call | tf_op jit(solution)/shard_map/backward_chain/pallas_call | solution.py:627
  177.9 38.4 %attention_back.1 = (bf16[1536,2048]{1,0:T(8,128)(2,1)}, bf16[4,512,512]{2,1,0:T(8,128)(2,1)}, f32[512,128]{1,0:T(8,128)}) custom-call(bf16[4,512,512]{2,1,0:T(8,128)(2,1)} %get-tuple-element.72.do_ref, f32[4,8,512]{2,1,0:T(8,128)} %get-tuple-element.73.dd_ref, bf16[4,512,512]{2,1,0:T(8,128)(2,1)} %get-tuple-element.74.dsm_ref, ...), custom_call_target="tpu_custom_call" | custom-call | tf_op jit(solution)/shard_map/attention_back/pallas_call | solution.py:658
  216.4 5.9 %fusion.38 = f32[512,1536]{1,0:T(8,128)S(1)} fusion(bf16[512,2048]{1,0:T(8,128)(2,1)S(1)} %copy-done.12, bf16[1536,2048]{1,0:T(8,128)(2,1)} %get-tuple-element.82), kind=kOutput, calls=%fused_computation.223 | convolution fusion | flops 3221225472 | bytes 11534336 | tf_op jit(solution)/shard_map/dot_general | solution.py:815
  224.6 2.1 convolution_convert_fusion.2
  229.3 2.6 convolution_bitcast_fusion
  232.6 2.4 fusion
  235.0 8.3 %convolution_convert_fusion.1 = bf16[512,2048]{1,0:T(8,128)(2,1)S(1)} fusion(bf16[512,2048]{1,0:T(8,128)(2,1)S(1)} %copy-done.9, bf16[2048,2048]{1,0:T(8,128)(2,1)} %get-tuple-element.88), kind=kOutput, calls=%fused_computation.10 | convolution fusion | flops 4296015872 | bytes 12582912 | tf_op jit(solution)/shard_map/dot_general | solution.py:815
  243.8 1.7 collective-permute-start.11
  247.8 5.2 %convolution_convert_fusion = bf16[2048,512]{1,0:T(8,128)(2,1)S(1)} fusion(bf16[2048,2048]{1,0:T(8,128)(2,1)S(1)} %bitcast.120, bf16[512,2048]{1,0:T(8,128)(2,1)S(1)} %copy-done.27), kind=kOutput, calls=%fused_computation.9 | convolution fusion | flops 4296015872 | bytes 12582912 | tf_op jit(solution)/shard_map/dot_general | solution.py:815
  254.5 3.9 collective-permute-done.10
  258.4 10.3 %collective-permute-done.11 = bf16[512,512]{1,0:T(8,128)(2,1)S(1)} collective-permute-done((bf16[512,512]{1,0:T(8,128)(2,1)S(1)}, bf16[512,512]{1,0:T(8,128)(2,1)S(1)}, u32[]{:S(2)}, u32[]{:S(2)}) %collective-permute-start.11) | collective-permute-done | bytes 524320 | tf_op jit(solution)/shard_map/ppermute | solution.py:680
  270.2 2.4 maximum_convert_fusion
  273.1 8.3 %collective-permute-done.5 = bf16[576,512]{1,0:T(8,128)(2,1)S(1)} collective-permute-done((bf16[576,512]{1,0:T(8,128)(2,1)S(1)}, bf16[576,512]{1,0:T(8,128)(2,1)S(1)}, u32[]{:S(2)}, u32[]{:S(2)}) %collective-permute-start.5) | collective-permute-done | bytes 589856 | tf_op jit(solution)/shard_map/ppermute | solution.py:680
  281.4 1.5 pad_maximum_fusion
  286.0 1.6 collective-permute-start.43
  289.8 1.7 collective-permute-start.13
  291.5 9.3 %collective-permute-done.43 = bf16[128,2048]{1,0:T(8,128)(2,1)S(1)} collective-permute-done((bf16[128,2048]{1,0:T(8,128)(2,1)S(1)}, bf16[128,2048]{1,0:T(8,128)(2,1)S(1)}, u32[]{:S(2)}, u32[]{:S(2)}) %collective-permute-start.43) | collective-permute-done | bytes 524320 | tf_op jit(solution)/shard_map/ppermute | solution.py:680
  301.5 9.9 %collective-permute-done.33 = bf16[512,512]{1,0:T(8,128)(2,1)S(1)} collective-permute-done((bf16[512,512]{1,0:T(8,128)(2,1)S(1)}, bf16[512,512]{1,0:T(8,128)(2,1)S(1)}, u32[]{:S(2)}, u32[]{:S(2)}) %collective-permute-start.33) | collective-permute-done | bytes 524320 | tf_op jit(solution)/shard_map/ppermute | solution.py:680
  312.1 1.8 collective-permute-start.24
  314.0 1.9 collective-permute-done.13
  316.0 1.6 collective-permute-start.14
  317.6 3.8 collective-permute-done.44
  321.5 1.6 collective-permute-start.45
  323.2 2.6 collective-permute-done.34
  325.9 1.6 collective-permute-start.35
  328.2 1.6 collective-permute-start.15
  330.0 2.7 collective-permute-start.46
  333.0 2.7 collective-permute-start.36
  335.7 1.6 collective-permute-done.25
  337.4 1.7 collective-permute-start.26
  339.2 2.4 collective-permute-start.47
  343.0 4.5 %collective-permute-done.26 = bf16[16,2048]{1,0:T(8,128)(2,1)S(1)} collective-permute-done((bf16[16,2048]{1,0:T(8,128)(2,1)S(1)}, bf16[16,2048]{1,0:T(8,128)(2,1)S(1)}, u32[]{:S(2)}, u32[]{:S(2)}) %collective-permute-start.26) | collective-permute-done | bytes 65568 | tf_op jit(solution)/shard_map/ppermute | solution.py:680
  347.7 3.0 collective-permute-start.16
  350.7 2.5 collective-permute-start.48
  353.4 1.8 collective-permute-done.16
  356.0 3.7 collective-permute-start.28
  360.6 2.5 collective-permute-start.18
  363.7 1.7 collective-permute-start.39
  365.5 1.5 collective-permute-start.29
  367.7 2.8 collective-permute-done.49
  370.6 2.7 collective-permute-start.50
  373.3 2.8 collective-permute-done.39
  376.3 2.7 collective-permute-start.40
  381.4 9.2 %collective-permute-done.50 = bf16[128,2048]{1,0:T(8,128)(2,1)S(1)} collective-permute-done((bf16[128,2048]{1,0:T(8,128)(2,1)S(1)}, bf16[128,2048]{1,0:T(8,128)(2,1)S(1)}, u32[]{:S(2)}, u32[]{:S(2)}) %collective-permute-start.50) | collective-permute-done | bytes 524320 | tf_op jit(solution)/shard_map/ppermute | solution.py:680
  391.0 5.2 %collective-permute-done.40 = bf16[512,512]{1,0:T(8,128)(2,1)S(1)} collective-permute-done((bf16[512,512]{1,0:T(8,128)(2,1)S(1)}, bf16[512,512]{1,0:T(8,128)(2,1)S(1)}, u32[]{:S(2)}, u32[]{:S(2)}) %collective-permute-start.40) | collective-permute-done | bytes 524320 | tf_op jit(solution)/shard_map/ppermute | solution.py:680
  399.8 2.1 fusion.3
  401.8 2.6 maximum_convert_fusion.2
  405.0 2.6 maximum_convert_fusion.1
  409.1 2.1 fusion.5
  (258 shorter events, 50.3 us)
Async XLA Ops:
  2.1 6.2 %copy-start.13 = (bf16[4,1,512,512]{3,2,1,0:T(8,128)(2,1)S(1)}, bf16[4,1,512,512]{3,2,1,0:T(8,128)(2,1)}, u32[]{:S(2)}) copy-start(bf16[4,1,512,512]{3,2,1,0:T(8,128)(2,1)} %param.28) | copy-start | bytes 6291460
  2.1 6.2 %copy-start.21 = (bf16[4,1,64,512]{3,2,1,0:T(8,128)(2,1)S(1)}, bf16[4,1,64,512]{3,2,1,0:T(8,128)(2,1)}, u32[]{:S(2)}) copy-start(bf16[4,1,64,512]{3,2,1,0:T(8,128)(2,1)} %param.29) | copy-start | bytes 786436
  5.2 20.8 %collective-permute-start = (bf16[528,512]{1,0:T(8,128)(2,1)}, bf16[528,512]{1,0:T(8,128)(2,1)}, u32[]{:S(2)}, u32[]{:S(2)}) collective-permute-start(bf16[528,512]{1,0:T(8,128)(2,1)} %get-tuple-element.147), channel_id=1, source_target_pairs={{0,8},{8,0},{16,24},{24,16},{1,9},{9,1},{17,25},{25,17},{2,10},{10... | collective-permute-start | bytes 1622024 | tf_op jit(solution)/shard_map/ppermute | solution.py:680
  5.7 20.7 %collective-permute-start.1 = (bf16[528,512]{1,0:T(8,128)(2,1)}, bf16[528,512]{1,0:T(8,128)(2,1)}, u32[]{:S(2)}, u32[]{:S(2)}) collective-permute-start(bf16[528,512]{1,0:T(8,128)(2,1)} %get-tuple-element.148), channel_id=1, source_target_pairs={{0,16},{8,24},{16,0},{24,8},{1,17},{9,25},{17,1},{25,9},{2,18},{10... | collective-permute-start | bytes 1622024 | tf_op jit(solution)/shard_map/ppermute | solution.py:680
  8.2 24.7 %collective-permute-start.2 = (bf16[528,512]{1,0:T(8,128)(2,1)}, bf16[528,512]{1,0:T(8,128)(2,1)}, u32[]{:S(2)}, u32[]{:S(2)}) collective-permute-start(bf16[528,512]{1,0:T(8,128)(2,1)} %get-tuple-element.149), channel_id=1, source_target_pairs={{0,24},{8,16},{16,8},{24,0},{1,25},{9,17},{17,9},{25,1},{2,26},{10... | collective-permute-start | bytes 1622024 | tf_op jit(solution)/shard_map/ppermute | solution.py:680
  9.9 115.5 %collective-permute-start.6 = (bf16[576,512]{1,0:T(8,128)(2,1)}, bf16[576,512]{1,0:T(8,128)(2,1)}, u32[]{:S(2)}, u32[]{:S(2)}) collective-permute-start(bf16[576,512]{1,0:T(8,128)(2,1)} %get-tuple-element.126), channel_id=1, source_target_pairs={{0,8},{8,0},{16,24},{24,16},{1,9},{9,1},{17,25},{25,17},{2,10},{10... | collective-permute-start | bytes 1769480 | tf_op jit(solution)/shard_map/ppermute | solution.py:680
  10.0 115.4 %collective-permute-start.7 = (bf16[576,512]{1,0:T(8,128)(2,1)}, bf16[576,512]{1,0:T(8,128)(2,1)}, u32[]{:S(2)}, u32[]{:S(2)}) collective-permute-start(bf16[576,512]{1,0:T(8,128)(2,1)} %get-tuple-element.127), channel_id=1, source_target_pairs={{0,16},{8,24},{16,0},{24,8},{1,17},{9,25},{17,1},{25,9},{2,18},{10... | collective-permute-start | bytes 1769480 | tf_op jit(solution)/shard_map/ppermute | solution.py:680
  14.6 4.0 copy-start.2
  20.3 12.6 %copy-start.4 = (bf16[1,528,512]{2,1,0:T(8,128)(2,1)S(1)}, bf16[1,528,512]{2,1,0:T(8,128)(2,1)}, u32[]{:S(2)}) copy-start(bf16[1,528,512]{2,1,0:T(8,128)(2,1)} %get-tuple-element.146) | copy-start | bytes 1622020
  26.1 99.3 %collective-permute-start.8 = (bf16[576,512]{1,0:T(8,128)(2,1)}, bf16[576,512]{1,0:T(8,128)(2,1)S(1)}, u32[]{:S(2)}, u32[]{:S(2)}) collective-permute-start(bf16[576,512]{1,0:T(8,128)(2,1)} %get-tuple-element.128), channel_id=1, source_target_pairs={{0,24},{8,16},{16,8},{24,0},{1,25},{9,17},{17,9},{25,1},{2,26},{10... | collective-permute-start | bytes 1769480 | tf_op jit(solution)/shard_map/ppermute | solution.py:680
  120.3 5.1 %copy-start.3 = (bf16[1,576,512]{2,1,0:T(8,128)(2,1)S(1)}, bf16[1,576,512]{2,1,0:T(8,128)(2,1)}, u32[]{:S(2)}) copy-start(bf16[1,576,512]{2,1,0:T(8,128)(2,1)} %get-tuple-element.125) | copy-start | bytes 1769476
  123.3 149.3 %collective-permute-start.3 = (bf16[576,512]{1,0:T(8,128)(2,1)}, bf16[576,512]{1,0:T(8,128)(2,1)}, u32[]{:S(2)}, u32[]{:S(2)}) collective-permute-start(bf16[576,512]{1,0:T(8,128)(2,1)} %get-tuple-element.136), channel_id=1, source_target_pairs={{0,8},{8,0},{16,24},{24,16},{1,9},{9,1},{17,25},{25,17},{2,10},{10... | collective-permute-start | bytes 1769480 | tf_op jit(solution)/shard_map/ppermute | solution.py:680
  123.5 149.1 %collective-permute-start.4 = (bf16[576,512]{1,0:T(8,128)(2,1)}, bf16[576,512]{1,0:T(8,128)(2,1)}, u32[]{:S(2)}, u32[]{:S(2)}) collective-permute-start(bf16[576,512]{1,0:T(8,128)(2,1)} %get-tuple-element.135), channel_id=1, source_target_pairs={{0,16},{8,24},{16,0},{24,8},{1,17},{9,25},{17,1},{25,9},{2,18},{10... | collective-permute-start | bytes 1769480 | tf_op jit(solution)/shard_map/ppermute | solution.py:680
  177.9 38.4 %copy-start.12 = (bf16[512,2048]{1,0:T(8,128)(2,1)S(1)}, bf16[512,2048]{1,0:T(8,128)(2,1)}, u32[]{:S(2)}) copy-start(bf16[512,2048]{1,0:T(8,128)(2,1)} %get-tuple-element.80.a1_ref) | copy-start | bytes 6291460
  216.4 6.0 %copy-start.6 = (bf16[4,512,64]{2,1,0:T(8,128)(2,1)S(1)}, bf16[4,512,64]{2,1,0:T(8,128)(2,1)}, u32[]{:S(2)}) copy-start(bf16[4,512,64]{2,1,0:T(8,128)(2,1)} %get-tuple-element.55.a1m_ref) | copy-start | bytes 786436
  216.4 6.0 %copy-start.15 = (bf16[4,1024,64]{2,1,0:T(8,128)(2,1)S(1)}, bf16[4,1024,64]{2,1,0:T(8,128)(2,1)}, u32[]{:S(2)}) copy-start(bf16[4,1024,64]{2,1,0:T(8,128)(2,1)} %get-tuple-element.83) | copy-start | bytes 1572868
  232.6 13.7 %slice-start = ((s8[8388608]{0:T(1024)(128)(4,1)}), s8[4194304]{0:T(1024)(128)(4,1)S(1)}, s32[]{:S(2)}) async-start(s8[8388608]{0:T(1024)(128)(4,1)} %bitcast.119), calls=%async_computation | async-start | bytes 8388608
  235.0 8.3 %copy-start.14 = (bf16[4,512,512]{2,1,0:T(8,128)(2,1)S(1)}, bf16[4,512,512]{2,1,0:T(8,128)(2,1)}, u32[]{:S(2)}) copy-start(bf16[4,512,512]{2,1,0:T(8,128)(2,1)} %get-tuple-element.81) | copy-start | bytes 6291460
  235.0 11.3 %slice-start.1 = ((s8[8388608]{0:T(1024)(128)(4,1)}), s8[4194304]{0:T(1024)(128)(4,1)S(1)}, s32[]{:S(2)}) async-start(s8[8388608]{0:T(1024)(128)(4,1)} %bitcast.119), calls=%async_computation.1 | async-start | bytes 8388608
  243.5 9.9 %collective-permute-start.9 = (bf16[512,512]{1,0:T(8,128)(2,1)S(1)}, bf16[512,512]{1,0:T(8,128)(2,1)S(1)}, u32[]{:S(2)}, u32[]{:S(2)}) collective-permute-start(bf16[512,512]{1,0:T(8,128)(2,1)S(1)} %get-tuple-element.163), channel_id=1, source_target_pairs={{0,8},{8,0},{16,24},{24,16},{1,9},{9,1},{17,25},{25,17},{2,10},{10... | collective-permute-start | bytes 1572872 | tf_op jit(solution)/shard_map/ppermute | solution.py:680
  243.6 14.8 %collective-permute-start.10 = (bf16[512,512]{1,0:T(8,128)(2,1)S(1)}, bf16[512,512]{1,0:T(8,128)(2,1)S(1)}, u32[]{:S(2)}, u32[]{:S(2)}) collective-permute-start(bf16[512,512]{1,0:T(8,128)(2,1)S(1)} %get-tuple-element.162), channel_id=1, source_target_pairs={{0,16},{8,24},{16,0},{24,8},{1,17},{9,25},{17,1},{25,9},{2,18},{10... | collective-permute-start | bytes 1572872 | tf_op jit(solution)/shard_map/ppermute | solution.py:680
  243.8 24.9 %collective-permute-start.11 = (bf16[512,512]{1,0:T(8,128)(2,1)S(1)}, bf16[512,512]{1,0:T(8,128)(2,1)S(1)}, u32[]{:S(2)}, u32[]{:S(2)}) collective-permute-start(bf16[512,512]{1,0:T(8,128)(2,1)S(1)} %get-tuple-element.161), channel_id=1, source_target_pairs={{0,24},{8,16},{16,8},{24,0},{1,25},{9,17},{17,9},{25,1},{2,26},{10... | collective-permute-start | bytes 1572872 | tf_op jit(solution)/shard_map/ppermute | solution.py:680
  247.8 5.2 %copy-start.20 = (bf16[512,512]{1,0:T(8,128)(2,1)S(1)}, bf16[512,512]{1,0:T(8,128)(2,1)}, u32[]{:S(2)}) copy-start(bf16[512,512]{1,0:T(8,128)(2,1)} %convolution_convert_fusion.2) | copy-start | bytes 1572868
  254.3 27.1 %collective-permute-start.5 = (bf16[576,512]{1,0:T(8,128)(2,1)S(1)}, bf16[576,512]{1,0:T(8,128)(2,1)S(1)}, u32[]{:S(2)}, u32[]{:S(2)}) collective-permute-start(bf16[576,512]{1,0:T(8,128)(2,1)S(1)} %copy-done.17), channel_id=1, source_target_pairs={{0,24},{8,16},{16,8},{24,0},{1,25},{9,17},{17,9},{25,1},{2,26},{10... | collective-permute-start | bytes 1769480 | tf_op jit(solution)/shard_map/ppermute | solution.py:680
  258.4 31.1 %collective-permute-start.12 = (bf16[256,2176]{1,0:T(8,128)(2,1)S(1)}, bf16[256,2176]{1,0:T(8,128)(2,1)S(1)}, u32[]{:S(2)}, u32[]{:S(2)}) collective-permute-start(bf16[256,2176]{1,0:T(8,128)(2,1)S(1)} %constant_dynamic-slice_fusion.19), channel_id=1, source_target_pairs={{0,8},{8,0},{16,24},{24,16},{1,9},{9,1},{17,25},{25,17},{2,10},{10... | collective-permute-start | bytes 3342344 | tf_op jit(solution)/shard_map/ppermute | solution.py:680
  268.7 16.8 %collective-permute-start.42 = (bf16[256,2048]{1,0:T(8,128)(2,1)S(1)}, bf16[256,2048]{1,0:T(8,128)(2,1)S(1)}, u32[]{:S(2)}, u32[]{:S(2)}) collective-permute-start(bf16[256,2048]{1,0:T(8,128)(2,1)S(1)} %constant_dynamic-slice_fusion.4), channel_id=1, source_target_pairs={{0,8},{8,0},{16,24},{24,16},{1,9},{9,1},{17,25},{25,17},{2,10},{10... | collective-permute-start | bytes 3145736 | tf_op jit(solution)/shard_map/ppermute | solution.py:680
  272.6 15.0 %collective-permute-start.32 = (bf16[1024,512]{1,0:T(8,128)(2,1)S(1)}, bf16[1024,512]{1,0:T(8,128)(2,1)S(1)}, u32[]{:S(2)}, u32[]{:S(2)}) collective-permute-start(bf16[1024,512]{1,0:T(8,128)(2,1)S(1)} %constant_dynamic-slice_fusion.9), channel_id=1, source_target_pairs={{0,8},{8,0},{16,24},{24,16},{1,9},{9,1},{17,25},{25,17},{2,10},{10... | collective-permute-start | bytes 3145736 | tf_op jit(solution)/shard_map/ppermute | solution.py:680
  272.6 15.9 %collective-permute-start.22 = (bf16[256,2048]{1,0:T(8,128)(2,1)S(1)}, bf16[256,2048]{1,0:T(8,128)(2,1)S(1)}, u32[]{:S(2)}, u32[]{:S(2)}) collective-permute-start(bf16[256,2048]{1,0:T(8,128)(2,1)S(1)} %constant_dynamic-slice_fusion.14), channel_id=1, source_target_pairs={{0,8},{8,0},{16,24},{24,16},{1,9},{9,1},{17,25},{25,17},{2,10},{10... | collective-permute-start | bytes 3145736 | tf_op jit(solution)/shard_map/ppermute | solution.py:680
  286.0 14.8 %collective-permute-start.43 = (bf16[128,2048]{1,0:T(8,128)(2,1)S(1)}, bf16[128,2048]{1,0:T(8,128)(2,1)S(1)}, u32[]{:S(2)}, u32[]{:S(2)}) collective-permute-start(bf16[128,2048]{1,0:T(8,128)(2,1)S(1)} %constant_dynamic-slice_fusion.3), channel_id=1, source_target_pairs={{0,1},{1,0},{2,3},{3,2},{4,5},{5,4},{6,7},{7,6},{8,9},{9,8},{10,11... | collective-permute-start | bytes 1572872 | tf_op jit(solution)/shard_map/ppermute | solution.py:680
  288.0 23.4 %collective-permute-start.33 = (bf16[512,512]{1,0:T(8,128)(2,1)S(1)}, bf16[512,512]{1,0:T(8,128)(2,1)S(1)}, u32[]{:S(2)}, u32[]{:S(2)}) collective-permute-start(bf16[512,512]{1,0:T(8,128)(2,1)S(1)} %constant_dynamic-slice_fusion.8), channel_id=1, source_target_pairs={{0,1},{1,0},{2,3},{3,2},{4,5},{5,4},{6,7},{7,6},{8,9},{9,8},{10,11... | collective-permute-start | bytes 1572872 | tf_op jit(solution)/shard_map/ppermute | solution.py:680
  289.0 23.0 %collective-permute-start.23 = (bf16[128,2048]{1,0:T(8,128)(2,1)S(1)}, bf16[128,2048]{1,0:T(8,128)(2,1)S(1)}, u32[]{:S(2)}, u32[]{:S(2)}) collective-permute-start(bf16[128,2048]{1,0:T(8,128)(2,1)S(1)} %constant_dynamic-slice_fusion.13), channel_id=1, source_target_pairs={{0,16},{8,24},{16,0},{24,8},{1,17},{9,25},{17,1},{25,9},{2,18},{10... | collective-permute-start | bytes 1572872 | tf_op jit(solution)/shard_map/ppermute | solution.py:680
  289.8 26.0 %collective-permute-start.13 = (bf16[128,2176]{1,0:T(8,128)(2,1)S(1)}, bf16[128,2176]{1,0:T(8,128)(2,1)S(1)}, u32[]{:S(2)}, u32[]{:S(2)}) collective-permute-start(bf16[128,2176]{1,0:T(8,128)(2,1)S(1)} %constant_dynamic-slice_fusion.18), channel_id=1, source_target_pairs={{0,16},{8,24},{16,0},{24,8},{1,17},{9,25},{17,1},{25,9},{2,18},{10... | collective-permute-start | bytes 1671176 | tf_op jit(solution)/shard_map/ppermute | solution.py:680
  301.0 20.4 %collective-permute-start.44 = (bf16[64,2048]{1,0:T(8,128)(2,1)S(1)}, bf16[64,2048]{1,0:T(8,128)(2,1)S(1)}, u32[]{:S(2)}, u32[]{:S(2)}) collective-permute-start(bf16[64,2048]{1,0:T(8,128)(2,1)S(1)} %constant_dynamic-slice_fusion.2), channel_id=1, source_target_pairs={{0,16},{8,24},{16,0},{24,8},{1,17},{9,25},{17,1},{25,9},{2,18},{10... | collective-permute-start | bytes 786440 | tf_op jit(solution)/shard_map/ppermute | solution.py:680
  311.6 14.2 %collective-permute-start.34 = (bf16[256,512]{1,0:T(8,128)(2,1)S(1)}, bf16[256,512]{1,0:T(8,128)(2,1)S(1)}, u32[]{:S(2)}, u32[]{:S(2)}) collective-permute-start(bf16[256,512]{1,0:T(8,128)(2,1)S(1)} %constant_dynamic-slice_fusion.7), channel_id=1, source_target_pairs={{0,16},{8,24},{16,0},{24,8},{1,17},{9,25},{17,1},{25,9},{2,18},{10... | collective-permute-start | bytes 786440 | tf_op jit(solution)/shard_map/ppermute | solution.py:680
  312.1 15.4 %collective-permute-start.24 = (bf16[64,2048]{1,0:T(8,128)(2,1)S(1)}, bf16[64,2048]{1,0:T(8,128)(2,1)S(1)}, u32[]{:S(2)}, u32[]{:S(2)}) collective-permute-start(bf16[64,2048]{1,0:T(8,128)(2,1)S(1)} %constant_dynamic-slice_fusion.12), channel_id=1, source_target_pairs={{0,1},{1,0},{2,3},{3,2},{4,5},{5,4},{6,7},{7,6},{8,9},{9,8},{10,11... | collective-permute-start | bytes 786440 | tf_op jit(solution)/shard_map/ppermute | solution.py:680
  316.0 12.1 %collective-permute-start.14 = (bf16[64,2176]{1,0:T(8,128)(2,1)S(1)}, bf16[64,2176]{1,0:T(8,128)(2,1)S(1)}, u32[]{:S(2)}, u32[]{:S(2)}) collective-permute-start(bf16[64,2176]{1,0:T(8,128)(2,1)S(1)} %constant_dynamic-slice_fusion.17), channel_id=1, source_target_pairs={{0,1},{1,0},{2,3},{3,2},{4,5},{5,4},{6,7},{7,6},{8,9},{9,8},{10,11... | collective-permute-start | bytes 835592 | tf_op jit(solution)/shard_map/ppermute | solution.py:680
  321.5 8.4 %collective-permute-start.45 = (bf16[32,2048]{1,0:T(8,128)(2,1)S(1)}, bf16[32,2048]{1,0:T(8,128)(2,1)S(1)}, u32[]{:S(2)}, u32[]{:S(2)}) collective-permute-start(bf16[32,2048]{1,0:T(8,128)(2,1)S(1)} %constant_dynamic-slice_fusion.1), channel_id=1, source_target_pairs={{0,2},{1,3},{2,0},{3,1},{4,6},{5,7},{6,4},{7,5},{8,10},{9,11},{10,... | collective-permute-start | bytes 393224 | tf_op jit(solution)/shard_map/ppermute | solution.py:680
  325.9 7.1 %collective-permute-start.35 = (bf16[128,512]{1,0:T(8,128)(2,1)S(1)}, bf16[128,512]{1,0:T(8,128)(2,1)S(1)}, u32[]{:S(2)}, u32[]{:S(2)}) collective-permute-start(bf16[128,512]{1,0:T(8,128)(2,1)S(1)} %constant_dynamic-slice_fusion.6), channel_id=1, source_target_pairs={{0,2},{1,3},{2,0},{3,1},{4,6},{5,7},{6,4},{7,5},{8,10},{9,11},{10,... | collective-permute-start | bytes 393224 | tf_op jit(solution)/shard_map/ppermute | solution.py:680
  327.6 9.7 %collective-permute-start.25 = (bf16[32,2048]{1,0:T(8,128)(2,1)S(1)}, bf16[32,2048]{1,0:T(8,128)(2,1)S(1)}, u32[]{:S(2)}, u32[]{:S(2)}) collective-permute-start(bf16[32,2048]{1,0:T(8,128)(2,1)S(1)} %constant_dynamic-slice_fusion.11), channel_id=1, source_target_pairs={{0,2},{1,3},{2,0},{3,1},{4,6},{5,7},{6,4},{7,5},{8,10},{9,11},{10,... | collective-permute-start | bytes 393224 | tf_op jit(solution)/shard_map/ppermute | solution.py:680
  328.2 19.4 %collective-permute-start.15 = (bf16[32,2176]{1,0:T(8,128)(2,1)S(1)}, bf16[32,2176]{1,0:T(8,128)(2,1)S(1)}, u32[]{:S(2)}, u32[]{:S(2)}) collective-permute-start(bf16[32,2176]{1,0:T(8,128)(2,1)S(1)} %constant_dynamic-slice_fusion.16), channel_id=1, source_target_pairs={{0,2},{1,3},{2,0},{3,1},{4,6},{5,7},{6,4},{7,5},{8,10},{9,11},{10,... | collective-permute-start | bytes 417800 | tf_op jit(solution)/shard_map/ppermute | solution.py:680
  330.0 9.2 %collective-permute-start.46 = (bf16[16,2048]{1,0:T(8,128)(2,1)S(1)}, bf16[16,2048]{1,0:T(8,128)(2,1)S(1)}, u32[]{:S(2)}, u32[]{:S(2)}) collective-permute-start(bf16[16,2048]{1,0:T(8,128)(2,1)S(1)} %constant_dynamic-slice_fusion), channel_id=1, source_target_pairs={{0,4},{1,5},{2,6},{3,7},{4,0},{5,1},{6,2},{7,3},{8,12},{9,13},{10,... | collective-permute-start | bytes 196616 | tf_op jit(solution)/shard_map/ppermute | solution.py:680
  333.0 8.6 %collective-permute-start.36 = (bf16[64,512]{1,0:T(8,128)(2,1)S(1)}, bf16[64,512]{1,0:T(8,128)(2,1)S(1)}, u32[]{:S(2)}, u32[]{:S(2)}) collective-permute-start(bf16[64,512]{1,0:T(8,128)(2,1)S(1)} %constant_dynamic-slice_fusion.5), channel_id=1, source_target_pairs={{0,4},{1,5},{2,6},{3,7},{4,0},{5,1},{6,2},{7,3},{8,12},{9,13},{10,... | collective-permute-start | bytes 196616 | tf_op jit(solution)/shard_map/ppermute | solution.py:680
  337.4 10.1 %collective-permute-start.26 = (bf16[16,2048]{1,0:T(8,128)(2,1)S(1)}, bf16[16,2048]{1,0:T(8,128)(2,1)S(1)}, u32[]{:S(2)}, u32[]{:S(2)}) collective-permute-start(bf16[16,2048]{1,0:T(8,128)(2,1)S(1)} %constant_dynamic-slice_fusion.10), channel_id=1, source_target_pairs={{0,4},{1,5},{2,6},{3,7},{4,0},{5,1},{6,2},{7,3},{8,12},{9,13},{10,... | collective-permute-start | bytes 196616 | tf_op jit(solution)/shard_map/ppermute | solution.py:680
  339.2 11.5 %collective-permute-start.47 = (bf16[16,2048]{1,0:T(8,128)(2,1)S(1)}, bf16[16,2048]{1,0:T(8,128)(2,1)S(1)}, u32[]{:S(2)}, u32[]{:S(2)}) collective-permute-start(bf16[16,2048]{1,0:T(8,128)(2,1)S(1)} %dynamic-slice_add_fusion.17), channel_id=1, source_target_pairs={{0,4},{1,5},{2,6},{3,7},{4,0},{5,1},{6,2},{7,3},{8,12},{9,13},{10,... | collective-permute-start | bytes 196616 | tf_op jit(solution)/shard_map/ppermute | solution.py:680
  341.6 11.6 %collective-permute-start.37 = (bf16[64,512]{1,0:T(8,128)(2,1)S(1)}, bf16[64,512]{1,0:T(8,128)(2,1)S(1)}, u32[]{:S(2)}, u32[]{:S(2)}) collective-permute-start(bf16[64,512]{1,0:T(8,128)(2,1)S(1)} %dynamic-slice_add_fusion.18), channel_id=1, source_target_pairs={{0,4},{1,5},{2,6},{3,7},{4,0},{5,1},{6,2},{7,3},{8,12},{9,13},{10,... | collective-permute-start | bytes 196616 | tf_op jit(solution)/shard_map/ppermute | solution.py:680
  347.5 5.8 %collective-permute-start.27 = (bf16[16,2048]{1,0:T(8,128)(2,1)S(1)}, bf16[16,2048]{1,0:T(8,128)(2,1)S(1)}, u32[]{:S(2)}, u32[]{:S(2)}) collective-permute-start(bf16[16,2048]{1,0:T(8,128)(2,1)S(1)} %dynamic-slice_add_fusion.19), channel_id=1, source_target_pairs={{0,4},{1,5},{2,6},{3,7},{4,0},{5,1},{6,2},{7,3},{8,12},{9,13},{10,... | collective-permute-start | bytes 196616 | tf_op jit(solution)/shard_map/ppermute | solution.py:680
  347.7 7.4 %collective-permute-start.16 = (bf16[16,2176]{1,0:T(8,128)(2,1)S(1)}, bf16[16,2176]{1,0:T(8,128)(2,1)S(1)}, u32[]{:S(2)}, u32[]{:S(2)}) collective-permute-start(bf16[16,2176]{1,0:T(8,128)(2,1)S(1)} %constant_dynamic-slice_fusion.15), channel_id=1, source_target_pairs={{0,4},{1,5},{2,6},{3,7},{4,0},{5,1},{6,2},{7,3},{8,12},{9,13},{10,... | collective-permute-start | bytes 208904 | tf_op jit(solution)/shard_map/ppermute | solution.py:680
  350.7 12.4 %collective-permute-start.48 = (bf16[32,2048]{1,0:T(8,128)(2,1)S(1)}, bf16[32,2048]{1,0:T(8,128)(2,1)S(1)}, u32[]{:S(2)}, u32[]{:S(2)}) collective-permute-start(bf16[32,2048]{1,0:T(8,128)(2,1)S(1)} %pad_maximum_fusion.28), channel_id=1, source_target_pairs={{0,2},{1,3},{2,0},{3,1},{4,6},{5,7},{6,4},{7,5},{8,10},{9,11},{10,... | collective-permute-start | bytes 393224 | tf_op jit(solution)/shard_map/ppermute | solution.py:680
  353.3 10.4 %collective-permute-start.38 = (bf16[128,512]{1,0:T(8,128)(2,1)S(1)}, bf16[128,512]{1,0:T(8,128)(2,1)S(1)}, u32[]{:S(2)}, u32[]{:S(2)}) collective-permute-start(bf16[128,512]{1,0:T(8,128)(2,1)S(1)} %pad_maximum_fusion.27), channel_id=1, source_target_pairs={{0,2},{1,3},{2,0},{3,1},{4,6},{5,7},{6,4},{7,5},{8,10},{9,11},{10,... | collective-permute-start | bytes 393224 | tf_op jit(solution)/shard_map/ppermute | solution.py:680
  355.2 5.4 %collective-permute-start.17 = (bf16[16,2176]{1,0:T(8,128)(2,1)S(1)}, bf16[16,2176]{1,0:T(8,128)(2,1)S(1)}, u32[]{:S(2)}, u32[]{:S(2)}) collective-permute-start(bf16[16,2176]{1,0:T(8,128)(2,1)S(1)} %dynamic-slice_add_fusion.16), channel_id=1, source_target_pairs={{0,4},{1,5},{2,6},{3,7},{4,0},{5,1},{6,2},{7,3},{8,12},{9,13},{10,... | collective-permute-start | bytes 208904 | tf_op jit(solution)/shard_map/ppermute | solution.py:680
  356.0 9.4 %collective-permute-start.28 = (bf16[32,2048]{1,0:T(8,128)(2,1)S(1)}, bf16[32,2048]{1,0:T(8,128)(2,1)S(1)}, u32[]{:S(2)}, u32[]{:S(2)}) collective-permute-start(bf16[32,2048]{1,0:T(8,128)(2,1)S(1)} %pad_maximum_fusion.26), channel_id=1, source_target_pairs={{0,2},{1,3},{2,0},{3,1},{4,6},{5,7},{6,4},{7,5},{8,10},{9,11},{10,... | collective-permute-start | bytes 393224 | tf_op jit(solution)/shard_map/ppermute | solution.py:680
  360.6 6.4 %collective-permute-start.18 = (bf16[32,2176]{1,0:T(8,128)(2,1)S(1)}, bf16[32,2176]{1,0:T(8,128)(2,1)S(1)}, u32[]{:S(2)}, u32[]{:S(2)}) collective-permute-start(bf16[32,2176]{1,0:T(8,128)(2,1)S(1)} %pad_maximum_fusion.25), channel_id=1, source_target_pairs={{0,2},{1,3},{2,0},{3,1},{4,6},{5,7},{6,4},{7,5},{8,10},{9,11},{10,... | collective-permute-start | bytes 417800 | tf_op jit(solution)/shard_map/ppermute | solution.py:680
  363.2 7.3 %collective-permute-start.49 = (bf16[64,2048]{1,0:T(8,128)(2,1)S(1)}, bf16[64,2048]{1,0:T(8,128)(2,1)S(1)}, u32[]{:S(2)}, u32[]{:S(2)}) collective-permute-start(bf16[64,2048]{1,0:T(8,128)(2,1)S(1)} %pad_maximum_fusion.24), channel_id=1, source_target_pairs={{0,16},{8,24},{16,0},{24,8},{1,17},{9,25},{17,1},{25,9},{2,18},{10... | collective-permute-start | bytes 786440 | tf_op jit(solution)/shard_map/ppermute | solution.py:680
  363.7 12.4 %collective-permute-start.39 = (bf16[256,512]{1,0:T(8,128)(2,1)S(1)}, bf16[256,512]{1,0:T(8,128)(2,1)S(1)}, u32[]{:S(2)}, u32[]{:S(2)}) collective-permute-start(bf16[256,512]{1,0:T(8,128)(2,1)S(1)} %pad_maximum_fusion.23), channel_id=1, source_target_pairs={{0,16},{8,24},{16,0},{24,8},{1,17},{9,25},{17,1},{25,9},{2,18},{10... | collective-permute-start | bytes 786440 | tf_op jit(solution)/shard_map/ppermute | solution.py:680
  365.5 13.4 %collective-permute-start.29 = (bf16[64,2048]{1,0:T(8,128)(2,1)S(1)}, bf16[64,2048]{1,0:T(8,128)(2,1)S(1)}, u32[]{:S(2)}, u32[]{:S(2)}) collective-permute-start(bf16[64,2048]{1,0:T(8,128)(2,1)S(1)} %pad_maximum_fusion.22), channel_id=1, source_target_pairs={{0,1},{1,0},{2,3},{3,2},{4,5},{5,4},{6,7},{7,6},{8,9},{9,8},{10,11... | collective-permute-start | bytes 786440 | tf_op jit(solution)/shard_map/ppermute | solution.py:680
  367.1 13.7 %collective-permute-start.19 = (bf16[64,2176]{1,0:T(8,128)(2,1)S(1)}, bf16[64,2176]{1,0:T(8,128)(2,1)S(1)}, u32[]{:S(2)}, u32[]{:S(2)}) collective-permute-start(bf16[64,2176]{1,0:T(8,128)(2,1)S(1)} %pad_maximum_fusion.21), channel_id=1, source_target_pairs={{0,1},{1,0},{2,3},{3,2},{4,5},{5,4},{6,7},{7,6},{8,9},{9,8},{10,11... | collective-permute-start | bytes 835592 | tf_op jit(solution)/shard_map/ppermute | solution.py:680
  370.6 19.9 %collective-permute-start.50 = (bf16[128,2048]{1,0:T(8,128)(2,1)S(1)}, bf16[128,2048]{1,0:T(8,128)(2,1)S(1)}, u32[]{:S(2)}, u32[]{:S(2)}) collective-permute-start(bf16[128,2048]{1,0:T(8,128)(2,1)S(1)} %pad_maximum_fusion.20), channel_id=1, source_target_pairs={{0,1},{1,0},{2,3},{3,2},{4,5},{5,4},{6,7},{7,6},{8,9},{9,8},{10,11... | collective-permute-start | bytes 1572872 | tf_op jit(solution)/shard_map/ppermute | solution.py:680
  376.3 19.9 %collective-permute-start.40 = (bf16[512,512]{1,0:T(8,128)(2,1)S(1)}, bf16[512,512]{1,0:T(8,128)(2,1)S(1)}, u32[]{:S(2)}, u32[]{:S(2)}) collective-permute-start(bf16[512,512]{1,0:T(8,128)(2,1)S(1)} %pad_maximum_fusion.19), channel_id=1, source_target_pairs={{0,1},{1,0},{2,3},{3,2},{4,5},{5,4},{6,7},{7,6},{8,9},{9,8},{10,11... | collective-permute-start | bytes 1572872 | tf_op jit(solution)/shard_map/ppermute | solution.py:680
  379.1 17.5 %collective-permute-start.30 = (bf16[128,2048]{1,0:T(8,128)(2,1)S(1)}, bf16[128,2048]{1,0:T(8,128)(2,1)S(1)}, u32[]{:S(2)}, u32[]{:S(2)}) collective-permute-start(bf16[128,2048]{1,0:T(8,128)(2,1)S(1)} %pad_maximum_fusion.18), channel_id=1, source_target_pairs={{0,16},{8,24},{16,0},{24,8},{1,17},{9,25},{17,1},{25,9},{2,18},{10... | collective-permute-start | bytes 1572872 | tf_op jit(solution)/shard_map/ppermute | solution.py:680
  380.9 16.6 %collective-permute-start.20 = (bf16[128,2176]{1,0:T(8,128)(2,1)S(1)}, bf16[128,2176]{1,0:T(8,128)(2,1)S(1)}, u32[]{:S(2)}, u32[]{:S(2)}) collective-permute-start(bf16[128,2176]{1,0:T(8,128)(2,1)S(1)} %pad_maximum_fusion.15), channel_id=1, source_target_pairs={{0,16},{8,24},{16,0},{24,8},{1,17},{9,25},{17,1},{25,9},{2,18},{10... | collective-permute-start | bytes 1671176 | tf_op jit(solution)/shard_map/ppermute | solution.py:680
  390.9 6.9 %collective-permute-start.51 = (bf16[256,2048]{1,0:T(8,128)(2,1)S(1)}, bf16[256,2048]{1,0:T(8,128)(2,1)S(1)}, u32[]{:S(2)}, u32[]{:S(2)}) collective-permute-start(bf16[256,2048]{1,0:T(8,128)(2,1)S(1)} %pad_maximum_fusion.14), channel_id=1, source_target_pairs={{0,8},{8,0},{16,24},{24,16},{1,9},{9,1},{17,25},{25,17},{2,10},{10... | collective-permute-start | bytes 3145736 | tf_op jit(solution)/shard_map/ppermute | solution.py:680
  396.5 2.9 collective-permute-start.41
  396.9 7.5 %collective-permute-start.31 = (bf16[256,2048]{1,0:T(8,128)(2,1)S(1)}, bf16[256,2048]{1,0:T(8,128)(2,1)S(1)}, u32[]{:S(2)}, u32[]{:S(2)}) collective-permute-start(bf16[256,2048]{1,0:T(8,128)(2,1)S(1)} %pad_maximum_fusion.12), channel_id=1, source_target_pairs={{0,8},{8,0},{16,24},{24,16},{1,9},{9,1},{17,25},{25,17},{2,10},{10... | collective-permute-start | bytes 3145736 | tf_op jit(solution)/shard_map/ppermute | solution.py:680
  397.8 9.8 %collective-permute-start.21 = (bf16[256,2176]{1,0:T(8,128)(2,1)S(1)}, bf16[256,2176]{1,0:T(8,128)(2,1)S(1)}, u32[]{:S(2)}, u32[]{:S(2)}) collective-permute-start(bf16[256,2176]{1,0:T(8,128)(2,1)S(1)} %pad_maximum_fusion.11), channel_id=1, source_target_pairs={{0,8},{8,0},{16,24},{24,16},{1,9},{9,1},{17,25},{25,17},{2,10},{10... | collective-permute-start | bytes 3342344 | tf_op jit(solution)/shard_map/ppermute | solution.py:680
  (19 other events, 48.6 us)
